TPU v7x, 32 devices: a whole 2x2x4 slice. The times are simulated.
32 devices in a mesh: dp: 8 (over z, y), tensor: 4 (over x, core).
Axes of the slice: x: 2, y: 2, z: 4, core: 2. Of those that a mesh axis runs over, the one named last changes fastest.
Arguments:
- hidden_in: bfloat16 [8192, 768], P(('dp', 'tensor')), may hold values from -6 to 6
- segment_ids: int32 [32, 256], P('dp'), may hold values from 0 to 7, never falling along the last dimension, each value on 1 to 96 neighbouring positions
- out_cotangent: bfloat16 [8192, 768], P(('dp', 'tensor')), may hold values from -18 to 18
- qkv_weight: bfloat16 [2, 768, 3, 768], P(None, None, None, 'tensor'), may hold values from -0.21875 to 0.21875
- qv_bias: bfloat16 [2, 2, 768], P(None, None, 'tensor'), may hold values from -1.796875 to 1.796875
- out_weight: bfloat16 [2, 768, 768], P(None, 'tensor'), may hold values from -0.875 to 0.875
- out_bias: bfloat16 [2, 768], replicated, may hold values from -1.796875 to 1.796875
- norm_gain: bfloat16 [2, 2, 768], replicated, may hold values from 0.5 to 1.5
- norm_bias: bfloat16 [2, 2, 768], replicated, may hold values from -1.796875 to 1.796875
- up_weight: bfloat16 [2, 768, 3072], P(None, None, 'tensor'), may hold values from -0.21875 to 0.21875
- up_bias: bfloat16 [2, 3072], P(None, 'tensor'), may hold values from -1.796875 to 1.796875
- down_weight: bfloat16 [2, 3072, 768], P(None, 'tensor'), may hold values from -0.109375 to 0.109375
- down_bias: bfloat16 [2, 768], replicated, may hold values from -1.796875 to 1.796875
Outputs:
- out_hidden: bfloat16 [8192, 768], P(('dp', 'tensor'))
- grad_hidden: float32 [8192, 768], P(('dp', 'tensor'))
- grad_qkv_weight: float32 [2, 768, 3, 768], P(None, None, None, 'tensor')
- grad_qv_bias: float32 [2, 2, 768], P(None, None, 'tensor')
- grad_out_weight: float32 [2, 768, 768], P(None, 'tensor')
- grad_out_bias: float32 [2, 768], replicated
- grad_norm_gain: float32 [2, 2, 768], replicated
- grad_norm_bias: float32 [2, 2, 768], replicated
- grad_up_weight: float32 [2, 768, 3072], P(None, None, 'tensor')
- grad_up_bias: float32 [2, 3072], P(None, 'tensor')
- grad_down_weight: float32 [2, 3072, 768], P(None, 'tensor')
- grad_down_bias: float32 [2, 768], replicated
All inputs are finite; a program needn't handle non-finite values.
Results may differ from a plain program's by a relative error of at most 0.033.
Values may be sent and summed in bfloat16 or wider, within the bound.
A program may use at most 128 MiB of HBM per device.

v0:
```python
import jax
import jax.numpy as jnp
from jax import lax
from jax.sharding import PartitionSpec as P

HEAD = 64


norm_eps = 1e-05


def gelu_tanh(pre_active):
    return jax.nn.gelu(pre_active, approximate=True)


def norm_forward(total, norm_gain, norm_shift):
    average = jnp.mean(total, axis=-1, keepdims=True)
    centered = total - average
    variance = jnp.mean(centered * centered, axis=-1, keepdims=True)
    inverse = lax.rsqrt(variance + norm_eps)
    scaled = centered * inverse
    return (scaled * norm_gain + norm_shift, scaled, inverse)


def norm_backward(incoming, scaled, inverse, norm_gain):
    gain_grad = jnp.sum(incoming * scaled, axis=0)
    shift_grad = jnp.sum(incoming, axis=0)
    inner = incoming * norm_gain
    result = inverse * (
        inner
        - jnp.mean(inner, axis=-1, keepdims=True)
        - scaled * jnp.mean(inner * scaled, axis=-1, keepdims=True)
    )
    return (result, gain_grad, shift_grad)


def sum_forward(full, weight):
    my_rows = full.shape[0] // lax.axis_size("tensor")

    def partial_value(offset, extent):
        return jnp.dot(full, weight, preferred_element_type=jnp.float32)

    return lax.psum_scatter(
        partial_value(jnp.int32(0), my_rows * lax.axis_size("tensor")).astype(jnp.bfloat16),
        "tensor",
        scatter_dimension=0,
        tiled=True,
    ).astype(jnp.float32)


def sum_backward(full, weight):
    my_rows = full.shape[0] // lax.axis_size("tensor")

    def partial_value(offset, extent):
        return jnp.einsum("nf,df->nd", full, weight, preferred_element_type=jnp.float32)

    return lax.psum_scatter(
        partial_value(jnp.int32(0), my_rows * lax.axis_size("tensor")).astype(jnp.bfloat16),
        "tensor",
        scatter_dimension=0,
        tiled=True,
    ).astype(jnp.float32)


def project_rows(context, out_weight):
    row_context = lax.all_to_all(context, "tensor", split_axis=0, concat_axis=1, tiled=True)
    return jnp.dot(
        row_context,
        lax.all_gather(out_weight, "tensor", axis=0, tiled=True),
        preferred_element_type=jnp.float32,
    )


def spread_rows(shard):
    return lax.all_gather(shard, "tensor", axis=0, tiled=True)


def spread_grads(shard):
    return lax.all_gather(shard, "tensor", axis=0, tiled=True)


def head_split(flat, sequences):
    return flat.reshape(sequences, -1, flat.shape[-1] // HEAD, HEAD)


def scores_of(query_heads, key_heads, allowed):
    raw_scores = jnp.einsum(
        "sqhe,skhe->shqk", query_heads, key_heads, preferred_element_type=jnp.float32
    ) * HEAD ** (-0.5)
    return jnp.where(allowed, raw_scores, -1000000000.0)


def layer_forward(tokens_now, sequences, allowed, weights):
    (
        qkv_weight,
        qv_bias,
        out_weight,
        out_bias,
        norm_gain,
        norm_shift,
        up_weight,
        up_bias,
        down_weight,
        down_bias,
    ) = weights
    local_width = qkv_weight.shape[-1]
    shard_in = tokens_now.astype(jnp.bfloat16)
    full_in = spread_rows(shard_in)
    projected = jnp.dot(
        full_in,
        qkv_weight.reshape(qkv_weight.shape[0], 3 * local_width),
        preferred_element_type=jnp.float32,
    )
    projected = projected.reshape(-1, 3, local_width)
    query_rows = (projected[:, 0] + qv_bias[0]).astype(jnp.bfloat16)
    key_rows = projected[:, 1].astype(jnp.bfloat16)
    value_rows = (projected[:, 2] + qv_bias[1]).astype(jnp.bfloat16)
    scores = scores_of(head_split(query_rows, sequences), head_split(key_rows, sequences), allowed)
    highest = jnp.max(scores, axis=-1, keepdims=True)
    log_total = highest + jnp.log(jnp.sum(jnp.exp(scores - highest), axis=-1, keepdims=True))
    probs_low = jnp.exp(scores - log_total).astype(jnp.bfloat16)
    context = jnp.einsum(
        "shqk,skhe->sqhe",
        probs_low,
        head_split(value_rows, sequences),
        preferred_element_type=jnp.float32,
    )
    context = context.reshape(-1, local_width).astype(jnp.bfloat16)
    attended = project_rows(context, out_weight) + out_bias
    normed, scaled_one, inverse_one = norm_forward(
        tokens_now + attended, norm_gain[0], norm_shift[0]
    )
    shard_mid = normed.astype(jnp.bfloat16)
    full_mid = spread_rows(shard_mid)
    pre_active = jnp.dot(full_mid, up_weight, preferred_element_type=jnp.float32) + up_bias
    active = gelu_tanh(pre_active).astype(jnp.bfloat16)
    lowered = sum_forward(active, down_weight) + down_bias
    result, scaled_two, inverse_two = norm_forward(normed + lowered, norm_gain[1], norm_shift[1])
    stored = (
        full_in,
        query_rows,
        key_rows,
        value_rows,
        log_total,
        context,
        scaled_one,
        inverse_one,
        full_mid,
        pre_active,
        active,
        scaled_two,
        inverse_two,
    )
    return (result, stored)


def layer_backward(incoming, sequences, allowed, weights, stored):
    (
        qkv_weight,
        qv_bias,
        out_weight,
        out_bias,
        norm_gain,
        norm_shift,
        up_weight,
        up_bias,
        down_weight,
        down_bias,
    ) = weights
    (
        stored_in,
        query_rows,
        key_rows,
        value_rows,
        log_total,
        context,
        scaled_one,
        inverse_one,
        stored_mid,
        pre_active,
        active,
        scaled_two,
        inverse_two,
    ) = stored
    local_width = qkv_weight.shape[-1]
    dsum_two, gain_two, shift_two = norm_backward(incoming, scaled_two, inverse_two, norm_gain[1])
    full_lowered = spread_grads(dsum_two.astype(jnp.bfloat16))
    grad_down_weight = jnp.einsum(
        "nf,nd->fd", active, full_lowered, preferred_element_type=jnp.float32
    )
    grad_down_bias = jnp.sum(full_lowered, axis=0, dtype=jnp.float32)
    grad_active = jnp.einsum(
        "nd,fd->nf", full_lowered, down_weight, preferred_element_type=jnp.float32
    )
    gelu_pull = jax.vjp(gelu_tanh, pre_active)[1]
    grad_pre = gelu_pull(grad_active)[0].astype(jnp.bfloat16)
    grad_up_weight = jnp.einsum(
        "nd,nf->df", stored_mid, grad_pre, preferred_element_type=jnp.float32
    )
    grad_up_bias = jnp.sum(grad_pre, axis=0, dtype=jnp.float32)
    grad_normed = dsum_two + sum_backward(grad_pre, up_weight)
    dsum_one, gain_one, shift_one = norm_backward(
        grad_normed, scaled_one, inverse_one, norm_gain[0]
    )
    full_attended = spread_grads(dsum_one.astype(jnp.bfloat16))
    grad_out_weight = jnp.einsum(
        "nf,nd->fd", context, full_attended, preferred_element_type=jnp.float32
    )
    grad_out_bias = jnp.sum(full_attended, axis=0, dtype=jnp.float32)
    grad_context = jnp.einsum(
        "nd,fd->nf", full_attended, out_weight, preferred_element_type=jnp.float32
    ).astype(jnp.bfloat16)
    grad_heads = head_split(grad_context, sequences)
    query_heads = head_split(query_rows, sequences)
    key_heads = head_split(key_rows, sequences)
    value_heads = head_split(value_rows, sequences)
    probs = jnp.exp(scores_of(query_heads, key_heads, allowed) - log_total)
    probs_low = probs.astype(jnp.bfloat16)
    grad_probs = jnp.einsum(
        "sqhe,skhe->shqk", grad_heads, value_heads, preferred_element_type=jnp.float32
    )
    grad_values = jnp.einsum(
        "shqk,sqhe->skhe", probs_low, grad_heads, preferred_element_type=jnp.float32
    )
    grad_scores = probs * (grad_probs - jnp.sum(grad_probs * probs, axis=-1, keepdims=True))
    grad_scores = grad_scores.astype(jnp.bfloat16)
    scale = HEAD ** (-0.5)
    grad_query = (
        jnp.einsum("shqk,skhe->sqhe", grad_scores, key_heads, preferred_element_type=jnp.float32)
        * scale
    )
    grad_keys = (
        jnp.einsum("shqk,sqhe->skhe", grad_scores, query_heads, preferred_element_type=jnp.float32)
        * scale
    )
    stacked = jnp.stack(
        [
            grad_query.reshape(-1, local_width),
            grad_keys.reshape(-1, local_width),
            grad_values.reshape(-1, local_width),
        ],
        axis=1,
    ).astype(jnp.bfloat16)
    grad_qkv_weight = jnp.einsum(
        "nd,ncf->dcf", stored_in, stacked, preferred_element_type=jnp.float32
    )
    grad_qv_bias = jnp.stack(
        [
            jnp.sum(stacked[:, 0], axis=0, dtype=jnp.float32),
            jnp.sum(stacked[:, 2], axis=0, dtype=jnp.float32),
        ]
    )
    grad_tokens = dsum_one + sum_backward(
        stacked.reshape(-1, 3 * local_width),
        qkv_weight.reshape(qkv_weight.shape[0], 3 * local_width),
    )
    grads = (
        grad_qkv_weight,
        grad_qv_bias,
        grad_out_weight,
        grad_out_bias,
        jnp.stack([gain_one, gain_two]),
        jnp.stack([shift_one, shift_two]),
        grad_up_weight,
        grad_up_bias,
        grad_down_weight,
        grad_down_bias,
    )
    return (grad_tokens, grads)


def final_sums(grads):
    summed = lax.psum(
        (grads[0], grads[1], grads[2], grads[3], grads[6], grads[7], grads[8], grads[9]), "dp"
    )
    norm_summed = lax.psum((grads[4], grads[5]), ("dp", "tensor"))
    return (
        summed[0],
        summed[1],
        summed[2],
        summed[3],
        norm_summed[0],
        norm_summed[1],
        summed[4],
        summed[5],
        summed[6],
        summed[7],
    )


def on_device(
    hidden_in,
    segment_ids,
    out_cotangent,
    qkv_weight,
    qv_bias,
    out_weight,
    out_bias,
    norm_gain,
    norm_bias,
    up_weight,
    up_bias,
    down_weight,
    down_bias,
):
    params = (
        qkv_weight,
        qv_bias,
        out_weight,
        out_bias,
        norm_gain,
        norm_bias,
        up_weight,
        up_bias,
        down_weight,
        down_bias,
    )
    layer_count = qkv_weight.shape[0]
    sequences = segment_ids.shape[0]
    allowed = (segment_ids[:, :, None] == segment_ids[:, None, :])[:, None]
    tokens_now = hidden_in.astype(jnp.float32)
    stored_all = []
    for layer_index in range(layer_count):
        weights = tuple((member[layer_index] for member in params))
        tokens_now, stored = layer_forward(tokens_now, sequences, allowed, weights)
        stored_all.append(stored)
    out_hidden = tokens_now.astype(jnp.bfloat16)
    gradient = out_cotangent.astype(jnp.float32)
    per_layer = [None] * layer_count
    for layer_index in reversed(range(layer_count)):
        weights = tuple((member[layer_index] for member in params))
        gradient, grads = layer_backward(
            gradient, sequences, allowed, weights, stored_all[layer_index]
        )
        per_layer[layer_index] = grads
    gathered = tuple(
        (
            jnp.stack([per_layer[layer_index][member] for layer_index in range(layer_count)])
            for member in range(10)
        )
    )
    gathered = final_sums(gathered)
    return (out_hidden, gradient) + tuple(gathered)


def solution(mesh):
    placed = (
        P(("dp", "tensor"), None),
        P("dp", None),
        P(("dp", "tensor"), None),
        P(None, None, None, "tensor"),
        P(None, None, "tensor"),
        P(None, "tensor", None),
        P(),
        P(),
        P(),
        P(None, None, "tensor"),
        P(None, "tensor"),
        P(None, "tensor", None),
        P(),
    )
    return jax.shard_map(
        on_device,
        mesh=mesh,
        in_specs=placed,
        out_specs=(
            P(("dp", "tensor"), None),
            P(("dp", "tensor"), None),
            P(None, None, None, "tensor"),
            P(None, None, "tensor"),
            P(None, "tensor", None),
            P(),
            P(),
            P(),
            P(None, None, "tensor"),
            P(None, "tensor"),
            P(None, "tensor", None),
            P(),
        ),
        check_vma=False,
    )
```

profile of v0, /device:TPU:0, one launch (start us, length us, event | category | flops | bytes accessed | tf_op | source)
XLA Modules:
  0.0 975.1 jit_solution(18216142386113718659)
XLA Ops:
  11.8 20.2 %all-gather.13.cloned.1.call-done = bf16[1024,768]{1,0:T(8,128)(2,1)} async-done(((bf16[256,768]{1,0:T(8,128)(2,1)}), bf16[1024,768]{1,0:T(8,128)(2,1)}) %all-gather.13.cloned.1.call-update) | async-done | bytes 1572880 | tf_op jit(solution)/shard_map/all_gather | solution.py:75
  32.0 2.8 fusion.22
  45.9 4.2 all-to-all-start
  51.6 6.1 all-to-all-done
  61.7 19.9 %all-gather.15.cloned.1.call-done = bf16[1024,768]{1,0:T(8,128)(2,1)} async-done(((bf16[256,768]{1,0:T(8,128)(2,1)}), bf16[1024,768]{1,0:T(8,128)(2,1)}) %all-gather.15.cloned.1.call-update) | async-done | bytes 1572880 | tf_op jit(solution)/shard_map/all_gather | solution.py:75
  81.6 3.3 fusion.54
  86.5 3.2 convolution_convert_fusion.5
  89.9 28.2 %reduce-scatter.7.cloned.1.call-done = bf16[256,768]{1,0:T(8,128)(2,1)} async-done(((bf16[1024,768]{1,0:T(8,128)(2,1)}), bf16[256,768]{1,0:T(8,128)(2,1)}) %reduce-scatter.7.cloned.1.call-update) | async-done | bytes 393232 | tf_op jit(solution)/shard_map/reduce_scatter | solution.py:43
  122.3 19.1 %all-gather.17.cloned.1.call-done = bf16[1024,768]{1,0:T(8,128)(2,1)} async-done(((bf16[256,768]{1,0:T(8,128)(2,1)}), bf16[1024,768]{1,0:T(8,128)(2,1)}) %all-gather.17.cloned.1.call-update) | async-done | bytes 1572880 | tf_op jit(solution)/shard_map/all_gather | solution.py:75
  141.4 2.7 fusion.18
  148.4 2.7 fusion.121
  151.1 2.4 squeeze.26
  153.5 2.4 squeeze.25
  160.5 4.1 all-to-all-start.1
  164.7 7.4 all-to-all-done.1
  176.3 19.8 %all-gather.19.cloned.1.call-done = bf16[1024,768]{1,0:T(8,128)(2,1)} async-done(((bf16[256,768]{1,0:T(8,128)(2,1)}), bf16[1024,768]{1,0:T(8,128)(2,1)}) %all-gather.19.cloned.1.call-update) | async-done | bytes 1572880 | tf_op jit(solution)/shard_map/all_gather | solution.py:75
  196.0 3.3 fusion.45
  201.0 3.3 convolution_convert_fusion.4
  204.3 28.2 %reduce-scatter.9.cloned.1.call-done = bf16[256,768]{1,0:T(8,128)(2,1)} async-done(((bf16[1024,768]{1,0:T(8,128)(2,1)}), bf16[256,768]{1,0:T(8,128)(2,1)}) %reduce-scatter.9.cloned.1.call-update) | async-done | bytes 393232 | tf_op jit(solution)/shard_map/reduce_scatter | solution.py:43
  237.9 19.3 %all-gather.21.cloned.1.call-done = bf16[1024,768]{1,0:T(8,128)(2,1)} async-done(((bf16[256,768]{1,0:T(8,128)(2,1)}), bf16[1024,768]{1,0:T(8,128)(2,1)}) %all-gather.21.cloned.1.call-update) | async-done | bytes 1572880 | tf_op jit(solution)/shard_map/all_gather | solution.py:79
  257.2 5.9 convert_reduce_fusion.2
  264.3 2.7 convolution_convert_fusion.3
  267.0 28.3 %reduce-scatter.11.cloned.1.call-done = bf16[256,768]{1,0:T(8,128)(2,1)} async-done(((bf16[1024,768]{1,0:T(8,128)(2,1)}), bf16[256,768]{1,0:T(8,128)(2,1)}) %reduce-scatter.11.cloned.1.call-update) | async-done | bytes 393232 | tf_op jit(solution)/shard_map/reduce_scatter | solution.py:57
  297.2 2.8 fusion.116
  300.1 2.8 fusion.123
  302.9 17.0 %all-gather.23.cloned.1.call-done = bf16[1024,768]{1,0:T(8,128)(2,1)} async-done(((bf16[256,768]{1,0:T(8,128)(2,1)}), bf16[1024,768]{1,0:T(8,128)(2,1)}) %all-gather.23.cloned.1.call-update) | async-done | bytes 1572880 | tf_op jit(solution)/shard_map/all_gather | solution.py:79
  319.9 2.9 convolution_convert_fusion.9
  324.8 3.1 fusion.33
  346.5 3.7 convolution_convert_fusion.1
  350.3 28.3 %reduce-scatter.13.cloned.1.call-done = bf16[256,768]{1,0:T(8,128)(2,1)} async-done(((bf16[1024,768]{1,0:T(8,128)(2,1)}), bf16[256,768]{1,0:T(8,128)(2,1)}) %reduce-scatter.13.cloned.1.call-update) | async-done | bytes 393232 | tf_op jit(solution)/shard_map/reduce_scatter | solution.py:57
  380.5 2.8 fusion.115
  383.5 19.6 %all-gather.25.cloned.1.call-done = bf16[1024,768]{1,0:T(8,128)(2,1)} async-done(((bf16[256,768]{1,0:T(8,128)(2,1)}), bf16[1024,768]{1,0:T(8,128)(2,1)}) %all-gather.25.cloned.1.call-update) | async-done | bytes 1572880 | tf_op jit(solution)/shard_map/all_gather | solution.py:79
  403.1 5.9 convert_reduce_fusion.3
  410.2 2.6 convolution_convert_fusion.2
  412.8 28.3 %reduce-scatter.15.cloned.1.call-done = bf16[256,768]{1,0:T(8,128)(2,1)} async-done(((bf16[1024,768]{1,0:T(8,128)(2,1)}), bf16[256,768]{1,0:T(8,128)(2,1)}) %reduce-scatter.15.cloned.1.call-update) | async-done | bytes 393232 | tf_op jit(solution)/shard_map/reduce_scatter | solution.py:57
  443.0 2.8 fusion.114
  450.3 5.3 convolution_bitcast_fusion
  455.6 10.1 %all-gather.27.cloned.1.call-done = bf16[1024,768]{1,0:T(8,128)(2,1)} async-done(((bf16[256,768]{1,0:T(8,128)(2,1)}), bf16[1024,768]{1,0:T(8,128)(2,1)}) %all-gather.27.cloned.1.call-update) | async-done | bytes 1572880 | tf_op jit(solution)/shard_map/all_gather | solution.py:79
  465.6 2.8 convolution_convert_fusion.7
  478.9 2.6 convolution_convert_fusion
  481.8 3.5 convolution_bitcast_fusion.2
  490.4 2.7 pad_maximum_fusion.1
  495.4 2.5 pad_maximum_fusion
  506.4 43.6 %all-reduce = (f32[2,2,768]{2,1,0:T(2,128)}, f32[2,2,768]{2,1,0:T(2,128)}) all-reduce(f32[2,2,768]{2,1,0:T(2,128)S(1)} %pad_maximum_fusion.5, f32[2,2,768]{2,1,0:T(2,128)S(1)} %pad_maximum_fusion.6), channel_id=1, replica_groups=mesh['dp'=8,'tensor'=4] {'dp','tensor'}, use_global_device_ids=true, to_apply=%region_42.43 | all-reduce | flops 6144 | bytes 49152 | tf_op jit(solution)/shard_map/psum | solution.py:276
  552.5 39.8 %all-reduce.1 = (f32[2,2,192]{2,1,0:T(2,128)}, f32[2,768]{1,0:T(2,128)}, f32[2,768]{1,0:T(2,128)}, f32[2,768]{1,0:T(2,128)}) all-reduce(f32[2,2,192]{2,1,0:T(2,128)S(1)} %pad_maximum_fusion.10, f32[2,768]{1,0:T(2,128)S(1)} %pad_maximum_fusion.7, f32[2,768]{1,0:T(2,128)S(1)} %pad_maximum_fusion.8, ...), channel_id=1, replica_groups=mesh['dp'=8,'tensor'=4] {'dp'}, use_global_device_ids=true, to_apply=%region_33.34 | all-reduce | flops 5376 | bytes 43008 | tf_op jit(solution)/shard_map/psum | solution.py:273
  594.3 362.8 %all-reduce.5.cloned.1.call-done = (f32[2,768,3,192]{1,3,2,0:T(8,128)}, f32[2,192,768]{2,1,0:T(8,128)}, f32[2,768,768]{2,1,0:T(8,128)}, f32[2,768,768]{2,1,0:T(8,128)}) async-done(((f32[2,768,3,192]{1,3,2,0:T(8,128)}, f32[2,192,768]{2,1,0:T(8,128)}, f32[2,768,768]{2,1,0:T(8,128)}, f32[2,768,768]{2,1,0:T(8,128)}), (f32[2,768,3,192]{1,3,2,0:T(8,128)}, f32[2,192,768]{2,1,0:T(8,128)}, f32[2,768,768]{2,1,0:T(8,128)}, ...) | async-done | bytes 14155792 | tf_op jit(solution)/shard_map/psum | solution.py:273
  957.0 4.4 copy.141
  962.4 2.4 copy.143
  (291 shorter events, 115.6 us)
Async XLA Ops:
  7.2 24.8 %all-gather.13.cloned.1.call-start = ((), (), s32[]{:S(2)}) async-start(), calls=%async_computation.8 | async-start | bytes 1966080 | tf_op jit(solution)/shard_map/all_gather | solution.py:75
  7.9 43.7 %all-gather.29.cloned.1.call-start = ((), (), s32[]{:S(2)}) async-start(), calls=%async_computation.22 | async-start | bytes 1474560 | tf_op jit(solution)/shard_map/all_gather | solution.py:69
  41.2 3.0 copy-start.15
  44.1 6.1 copy-start.39
  44.1 6.1 copy-start.37
  44.2 6.1 copy-start.38
  45.9 15.7 %copy-start.40 = (bf16[2,768]{1,0:T(2,128)(2,1)S(1)}, bf16[2,768]{1,0:T(2,128)(2,1)}, u32[]{:S(2)}) copy-start(bf16[2,768]{1,0:T(2,128)(2,1)} %param.23) | copy-start | bytes 9220
  45.9 11.8 %all-to-all-start = ((bf16[4,256,192]{1,2,0:T(8,128)(2,1)}), bf16[4,256,192]{1,2,0:T(8,128)(2,1)}, u32[]{:S(2)}, u32[]{:S(2)}) async-start(bf16[4,256,192]{1,2,0:T(8,128)(2,1)} %bitcast.204), calls=%async_computation | async-start | bytes 786432 | tf_op jit(solution)/shard_map/all_to_all | solution.py:66
  50.2 31.4 %all-gather.15.cloned.1.call-start = ((), (), s32[]{:S(2)}) async-start(), calls=%async_computation.9 | async-start | bytes 1966080 | tf_op jit(solution)/shard_map/all_gather | solution.py:75
  61.6 56.5 %reduce-scatter.7.cloned.1.call-start = ((), (), s32[]{:S(2)}) async-start(), calls=%async_computation.10 | async-start | bytes 1966080 | tf_op jit(solution)/shard_map/reduce_scatter | solution.py:43
  81.6 5.0 copy-start.42
  86.5 3.3 copy-start.41
  89.8 51.6 %all-gather.17.cloned.1.call-start = ((), (), s32[]{:S(2)}) async-start(), calls=%async_computation.11 | async-start | bytes 1966080 | tf_op jit(solution)/shard_map/all_gather | solution.py:75
  121.6 43.1 %all-gather.31.cloned.1.call-start = ((), (), s32[]{:S(2)}) async-start(), calls=%async_computation.23 | async-start | bytes 1474560 | tf_op jit(solution)/shard_map/all_gather | solution.py:69
  155.8 2.9 copy-start.17
  160.5 11.6 %all-to-all-start.1 = ((bf16[4,256,192]{1,2,0:T(8,128)(2,1)}), bf16[4,256,192]{1,2,0:T(8,128)(2,1)}, u32[]{:S(2)}, u32[]{:S(2)}) async-start(bf16[4,256,192]{1,2,0:T(8,128)(2,1)} %bitcast.206), calls=%async_computation.2 | async-start | bytes 786432 | tf_op jit(solution)/shard_map/all_to_all | solution.py:66
  164.6 31.4 %all-gather.19.cloned.1.call-start = ((), (), s32[]{:S(2)}) async-start(), calls=%async_computation.12 | async-start | bytes 1966080 | tf_op jit(solution)/shard_map/all_gather | solution.py:75
  176.2 56.4 %reduce-scatter.9.cloned.1.call-start = ((), (), s32[]{:S(2)}) async-start(), calls=%async_computation.13 | async-start | bytes 1966080 | tf_op jit(solution)/shard_map/reduce_scatter | solution.py:43
  196.0 5.0 copy-start.43
  204.3 53.0 %all-gather.21.cloned.1.call-start = ((), (), s32[]{:S(2)}) async-start(), calls=%async_computation.14 | async-start | bytes 1966080 | tf_op jit(solution)/shard_map/all_gather | solution.py:79
  232.6 3.3 copy-start.30
  237.4 57.9 %reduce-scatter.11.cloned.1.call-start = ((), (), s32[]{:S(2)}) async-start(), calls=%async_computation.15 | async-start | bytes 1966080 | tf_op jit(solution)/shard_map/reduce_scatter | solution.py:57
  257.2 7.0 copy-start.44
  267.0 52.9 %all-gather.23.cloned.1.call-start = ((), (), s32[]{:S(2)}) async-start(), calls=%async_computation.16 | async-start | bytes 1966080 | tf_op jit(solution)/shard_map/all_gather | solution.py:79
  300.1 78.5 %reduce-scatter.13.cloned.1.call-start = ((), (), s32[]{:S(2)}) async-start(), calls=%async_computation.17 | async-start | bytes 1966080 | tf_op jit(solution)/shard_map/reduce_scatter | solution.py:57
  324.8 3.1 copy-start.1
  324.8 3.1 copy-start.18
  324.8 3.2 copy-start.23
  350.2 52.9 %all-gather.25.cloned.1.call-start = ((), (), s32[]{:S(2)}) async-start(), calls=%async_computation.18 | async-start | bytes 1966080 | tf_op jit(solution)/shard_map/all_gather | solution.py:79
  383.3 57.8 %reduce-scatter.15.cloned.1.call-start = ((), (), s32[]{:S(2)}) async-start(), calls=%async_computation.19 | async-start | bytes 1966080 | tf_op jit(solution)/shard_map/reduce_scatter | solution.py:57
  403.1 7.1 copy-start.45
  412.8 52.9 %all-gather.27.cloned.1.call-start = ((), (), s32[]{:S(2)}) async-start(), calls=%async_computation.20 | async-start | bytes 1966080 | tf_op jit(solution)/shard_map/all_gather | solution.py:79
  445.8 146.5 %reduce-scatter.17.cloned.1.call-start = ((), (), s32[]{:S(2)}) async-start(), calls=%async_computation.21 | async-start | bytes 1966080 | tf_op jit(solution)/shard_map/reduce_scatter | solution.py:57
  445.9 4.4 copy-start.25
  476.6 4.9 copy-start.13
  477.2 4.3 copy-start.14
  481.5 3.8 copy-start.7
  481.5 3.8 copy-start.29
  481.5 475.5 %all-reduce.5.cloned.1.call-start = ((), (), s32[]{:S(2)}) async-start(), calls=%async_computation.24 | async-start | bytes 28311552 | tf_op jit(solution)/shard_map/psum | solution.py:273
  481.8 4.0 copy-start.32
  481.8 4.0 copy-start.48
  490.4 3.5 copy-start.54
  505.6 86.7 %copy-start.19 = (f32[256,768]{1,0:T(8,128)S(1)}, f32[256,768]{1,0:T(8,128)}, u32[]{:S(2)}) copy-start(f32[256,768]{1,0:T(8,128)} %get-tuple-element.57) | copy-start | bytes 2359300
  957.0 5.4 slice-start.2
  957.0 4.4 copy-start.33
  957.0 5.4 slice-start.3
  961.4 4.2 slice-start
  962.4 3.5 slice-start.1
  (30 other events, 53.8 us)
Sparse Core Ops, SparseCore 0:
  9.6 22.3 all-gather.12
  34.1 17.4 all-gather.28
  61.7 19.7 all-gather.14
  89.9 28.1 reduce-scatter.6
  121.7 19.6 all-gather.16
  142.9 17.4 all-gather.30
  176.3 19.6 all-gather.18
  204.4 28.1 reduce-scatter.8
  237.5 19.6 all-gather.20
  267.1 28.1 reduce-scatter.10
  300.2 19.6 all-gather.22
  350.4 28.1 reduce-scatter.12
  383.4 19.6 all-gather.24
  412.9 28.1 reduce-scatter.14
  445.9 19.6 all-gather.26
  481.6 28.1 reduce-scatter.16
  515.5 441.4 all-reduce.4
where the time goes:
time: 984 us; the launch traced here: 975 us
  waiting for transfers between devices  665 us (68%)
  matrix products  86 us (9%)
  blocking collectives  83.3 us (8%)
  local copies, waits for them, and re-layouts  69.1 us (7%)
  other arithmetic  46.3 us (5%)
  between operations  15.4 us (2%)
  starting transfers between devices  10.1 us (1%)
    psum x1, waiting for transfers between devices, final_sums(): lax.psum((grads[0], grads[1], grads[2], grads[3], grads[6], grads[7], gra...  363 us
    reduce_scatter x4, waiting for transfers between devices, sum_backward(): lax.psum_scatter(partial_value(jnp.int32(0), my_rows * lax.axis_size('ten...  84.8 us
    all_gather x4, waiting for transfers between devices, spread_rows(): return lax.all_gather(shard, 'tensor', axis=0, tiled=True)  78.9 us
    all_gather x4, waiting for transfers between devices, spread_grads(): return lax.all_gather(shard, 'tensor', axis=0, tiled=True)  66 us
    reduce_scatter x2, waiting for transfers between devices, sum_forward(): lax.psum_scatter(partial_value(jnp.int32(0), my_rows * lax.axis_size('ten...  56.5 us
    psum x1, blocking collectives, final_sums(): norm_summed = lax.psum((grads[4], grads[5]), ('dp', 'tensor'))  43.6 us
    psum x1, blocking collectives, final_sums(): lax.psum((grads[0], grads[1], grads[2], grads[3], grads[6], grads[7], gra...  39.8 us
    unnamed x126, local copies, waits for them, and re-layouts  28.8 us
  transfers between devices with their start and end apart: 19, of which 17 were waited for; matrix products, arithmetic and copies ran while one was open for 7% of the time, Pallas kernels for 0%

commit v1 on v0

--- a/solution.py
+++ b/solution.py
@@ -1,9 +1,274 @@
 import jax
 import jax.numpy as jnp
 from jax import lax
+from jax.experimental import pallas as pl
+from jax.experimental.pallas import tpu as pltpu
 from jax.sharding import PartitionSpec as P
 
 HEAD = 64
+MESH = pl.DeviceIdType.MESH
+Y_SIZE = 2
+Z_SIZE = 4
+GROUP = Y_SIZE * Z_SIZE
+F32 = jnp.float32
+BF16 = jnp.bfloat16
+
+
+class Place:
+    def __init__(self):
+        self.dp = lax.axis_index("dp")
+        self.t = lax.axis_index("tensor")
+        inner = lax.rem(self.dp, GROUP)
+        base = self.dp - inner
+        self.y = lax.rem(inner, Y_SIZE)
+        self.z = inner // Y_SIZE
+        z_pair = self.z + 1 - 2 * lax.rem(self.z, 2)
+        z_mid = Z_SIZE - 1 - self.z
+        self.is_end = jnp.logical_or(self.z == 0, self.z == Z_SIZE - 1)
+        self.is_inner = jnp.logical_not(self.is_end)
+        self.core = (self.dp, self.t + 1 - 2 * lax.rem(self.t, 2))
+        self.over = (self.dp, lax.rem(self.t + 2, 4))
+        self.y_pair = (base + self.z * Y_SIZE + 1 - self.y, self.t)
+        self.z_pair = (base + z_pair * Y_SIZE + self.y, self.t)
+        self.z_mid = (base + z_mid * Y_SIZE + self.y, self.t)
+
+
+class Links:
+    def __init__(self, sems):
+        self.sems = sems
+        self.used = 0
+
+    def copy(self, src, dst, device):
+        at = self.used
+        self.used += 1
+        return pltpu.make_async_remote_copy(
+            src_ref=src,
+            dst_ref=dst,
+            send_sem=self.sems.at[0, at],
+            recv_sem=self.sems.at[1, at],
+            device_id=device,
+            device_id_type=MESH,
+        )
+
+
+def greet(devices):
+    barrier = pltpu.get_barrier_semaphore()
+    for device in devices:
+        pl.semaphore_signal(barrier, inc=1, device_id=device, device_id_type=MESH)
+    pl.semaphore_wait(barrier, len(devices))
+
+
+def added(one, two, dtype):
+    return (one.astype(F32) + two.astype(F32)).astype(dtype)
+
+
+def sum_item(place, links, mine, landing, result, start, size):
+    from_y, from_z, from_mid = landing.at[0], landing.at[1], landing.at[2]
+    half = mine.shape[0] // 2
+    here = pl.ds(pl.multiple_of(place.y * half + start, 16), size)
+    there = pl.ds(pl.multiple_of((1 - place.y) * half + start, 16), size)
+    part = pl.ds(start, size)
+    dtype = mine.dtype
+    y_out = links.copy(mine.at[there], from_y.at[part], place.y_pair)
+    pair_in = links.copy(mine.at[here], from_z.at[part], place.z_pair)
+    mid = links.copy(mine.at[here], from_mid.at[part], place.z_mid)
+    pair_out = links.copy(result.at[here], from_z.at[part], place.z_pair)
+    y_back = links.copy(result.at[here], result.at[here], place.y_pair)
+    y_out.start()
+    yield
+    y_out.wait_recv()
+    mine[here] = added(mine[here], from_y[part], dtype)
+
+    @pl.when(place.is_end)
+    def _():
+        pair_in.start()
+
+    yield
+
+    @pl.when(place.is_inner)
+    def _():
+        pair_in.wait_recv()
+        mine[here] = added(mine[here], from_z[part], dtype)
+        mid.start()
+
+    yield
+
+    @pl.when(place.is_inner)
+    def _():
+        mid.wait_recv()
+        result[here] = added(mine[here], from_mid[part], dtype)
+        pair_out.start()
+        y_back.start()
+
+    yield
+
+    @pl.when(place.is_end)
+    def _():
+        pair_out.wait_recv()
+        result[here] = from_z[part]
+        y_back.start()
+
+    yield
+    yield
+    y_back.wait_recv()
+    y_out.wait_send()
+    y_back.wait_send()
+
+    @pl.when(place.is_end)
+    def _():
+        pair_in.wait_send()
+
+    @pl.when(place.is_inner)
+    def _():
+        mid.wait_send()
+        pair_out.wait_send()
+
+
+def small_item(place, links, mine, steps, landing, result):
+    top = pl.ds(0, 8)
+    steps[0] = mine[...]
+    near = links.copy(steps.at[0, top], landing.at[0, top], place.core)
+    near.start()
+    yield
+    near.wait_recv()
+    steps[1] = steps[0]
+    steps[1, top] = steps[0, top] + landing[0, top]
+    over = links.copy(steps.at[1, top], landing.at[1, top], place.over)
+    over.start()
+    yield
+    over.wait_recv()
+    steps[2] = steps[1]
+    steps[2, top] = steps[1, top] + landing[1, top]
+    across = links.copy(steps.at[2], landing.at[2], place.y_pair)
+    across.start()
+    yield
+    across.wait_recv()
+    steps[3] = steps[2] + landing[2]
+    pair_in = links.copy(steps.at[3], landing.at[3], place.z_pair)
+    mid = links.copy(steps.at[4], landing.at[4], place.z_mid)
+    pair_out = links.copy(result, landing.at[3], place.z_pair)
+
+    @pl.when(place.is_end)
+    def _():
+        pair_in.start()
+
+    yield
+
+    @pl.when(place.is_inner)
+    def _():
+        pair_in.wait_recv()
+        steps[4] = steps[3] + landing[3]
+        mid.start()
+
+    yield
+
+    @pl.when(place.is_inner)
+    def _():
+        mid.wait_recv()
+        result[...] = steps[4] + landing[4]
+        pair_out.start()
+
+    yield
+
+    @pl.when(place.is_end)
+    def _():
+        pair_out.wait_recv()
+        result[...] = landing[3]
+
+    yield
+    near.wait_send()
+    over.wait_send()
+    across.wait_send()
+
+    @pl.when(place.is_end)
+    def _():
+        pair_in.wait_send()
+
+    @pl.when(place.is_inner)
+    def _():
+        mid.wait_send()
+        pair_out.wait_send()
+
+
+class Ticker:
+    def __init__(self):
+        self.waiting = []
+        self.running = []
+
+    def add(self, items):
+        self.waiting.extend(items)
+
+    def tick(self, enter=1):
+        for _ in range(enter):
+            if self.waiting:
+                self.running.append(self.waiting.pop(0))
+        left = []
+        for item in self.running:
+            try:
+                next(item)
+                left.append(item)
+            except StopIteration:
+                pass
+        self.running = left
+
+    def finish(self):
+        while self.waiting or self.running:
+            self.tick()
+
+
+def chunked(place, links, mine, landing, result, size):
+    half = mine.shape[0] // 2
+    return [
+        sum_item(place, links, mine, landing, result, start, size)
+        for start in range(0, half, size)
+    ]
+
+
+def sum_kernel(small, down, up, qkv, out, small_sum, down_sum, up_sum, qkv_sum, out_sum,
+               own_small, land_small, own_down, land_down, own_up, land_up, own_qkv, land_qkv, own_out, land_out, sems):
+    place = Place()
+    links = Links(sems)
+    greet((place.core, place.over, place.y_pair, place.z_pair, place.z_mid))
+    ticker = Ticker()
+    ticker.add([small_item(place, links, small, own_small, land_small, small_sum)])
+    for source, own, landing, result, size in (
+        (down, own_down, land_down, down_sum, 96),
+        (up, own_up, land_up, up_sum, 96),
+        (qkv, own_qkv, land_qkv, qkv_sum, 96),
+        (out, own_out, land_out, out_sum, 96),
+    ):
+        own[...] = source[...]
+        ticker.add(chunked(place, links, own, landing, result, size))
+    ticker.tick(6)
+    ticker.finish()
+
+
+def sum_over_group(small, down, up, qkv, out, which):
+    arrays = (small, down, up, qkv, out)
+    scratch = [pltpu.VMEM((5,) + small.shape, F32), pltpu.VMEM((5,) + small.shape, F32)]
+    for array in arrays[1:]:
+        half = (array.shape[0] // 2, array.shape[1])
+        scratch += [pltpu.VMEM(array.shape, BF16), pltpu.VMEM((3,) + half, BF16)]
+    scratch.append(pltpu.SemaphoreType.DMA((2, 128)))
+    vmem = pl.BlockSpec(memory_space=pltpu.VMEM)
+    return pl.pallas_call(
+        sum_kernel,
+        out_shape=[jax.ShapeDtypeStruct(array.shape, array.dtype) for array in arrays],
+        in_specs=[vmem] * 5,
+        out_specs=[vmem] * 5,
+        scratch_shapes=scratch,
+        compiler_params=pltpu.CompilerParams(
+            collective_id=which, has_side_effects=True, vmem_limit_bytes=56 << 20
+        ),
+    )(*arrays)
+
+
+def over_outer_groups(values):
+    size = lax.axis_size("dp")
+    if size == GROUP:
+        return values
+    groups = [[first + GROUP * turn for turn in range(size // GROUP)] for first in range(GROUP)]
+    return [lax.psum(value, "dp", axis_index_groups=groups) for value in values]
 
 
 norm_eps = 1e-05
@@ -269,22 +534,48 @@
     return (grad_tokens, grads)
 
 
-def final_sums(grads):
-    summed = lax.psum(
-        (grads[0], grads[1], grads[2], grads[3], grads[6], grads[7], grads[8], grads[9]), "dp"
-    )
-    norm_summed = lax.psum((grads[4], grads[5]), ("dp", "tensor"))
-    return (
-        summed[0],
-        summed[1],
-        summed[2],
-        summed[3],
-        norm_summed[0],
-        norm_summed[1],
-        summed[4],
-        summed[5],
-        summed[6],
-        summed[7],
+def final_sums(per_layer):
+    summed = []
+    for layer_index, grads in enumerate(per_layer):
+        width = grads[8].shape[-1]
+        local = grads[1].shape[-1]
+        quarter = 1.0 / lax.axis_size("tensor")
+        small = jnp.concatenate(
+            [
+                grads[4],
+                grads[5],
+                grads[3][None] * quarter,
+                grads[9][None] * quarter,
+                jnp.zeros((2, width), F32),
+                grads[7][None],
+                jnp.pad(grads[1], ((0, 0), (0, width - local))),
+                jnp.zeros((5, width), F32),
+            ]
+        )
+        big = [
+            member.reshape(member.shape[0], -1).astype(BF16)
+            for member in (grads[8], grads[6], grads[0], grads[2])
+        ]
+        done = sum_over_group(small, *big, which=layer_index)
+        done = over_outer_groups(list(done))
+        small, down, up, qkv, out = done
+        summed.append(
+            (
+                qkv.reshape(qkv.shape[0], 3, -1).astype(F32),
+                small[9:11, :local],
+                out.astype(F32),
+                small[4],
+                small[0:2],
+                small[2:4],
+                up.astype(F32),
+                small[8],
+                down.astype(F32),
+                small[5],
+            )
+        )
+    return tuple(
+        jnp.stack([summed[layer_index][member] for layer_index in range(len(summed))])
+        for member in range(10)
     )
 
 
@@ -333,13 +624,7 @@
             gradient, sequences, allowed, weights, stored_all[layer_index]
         )
         per_layer[layer_index] = grads
-    gathered = tuple(
-        (
-            jnp.stack([per_layer[layer_index][member] for layer_index in range(layer_count)])
-            for member in range(10)
-        )
-    )
-    gathered = final_sums(gathered)
+    gathered = final_sums(per_layer)
     return (out_hidden, gradient) + tuple(gathered)
 
 

time: 984 us -> 729 us (0.74)
  waiting for transfers between devices: 665 us -> 279 us
  Pallas kernels: 0 us -> 199 us
  blocking collectives: 83.3 us -> 0 us
    psum x1 -> x0, waiting for transfers between devices: 363 us -> none  [final_sums(): lax.psum((grads[0], grads[1], grads[2], grads[3], grads[6], grads[7], gra...]
    pallas_call x0 -> x2, Pallas kernels: none -> 199 us  [sum_over_group(): pl.pallas_call(sum_kernel, out_shape=[jax.ShapeDtypeStruct(array.shape, a...]
    psum x2 -> x0, blocking collectives: 83.3 us -> none  [the longest x1 43.6 us: final_sums(): norm_summed = lax.psum((grads[4], grads[5]), ('dp', 'tensor'))]
    unnamed x126 -> x108, local copies, waits for them, and re-layouts: 28.8 us -> 14.7 us
    reduce_scatter x4, waiting for transfers between devices: 84.8 us -> 71.6 us  [sum_backward(): lax.psum_scatter(partial_value(jnp.int32(0), my_rows * lax.axis_size('ten...]
    all_gather x4, waiting for transfers between devices: 66 us -> 55.9 us  [spread_grads(): return lax.all_gather(shard, 'tensor', axis=0, tiled=True)]
  transfers between devices with their start and end apart: 19 -> 18, of which waited for: 17 -> 15; matrix products, arithmetic and copies ran while one was open for 7% -> 14% of each run, Pallas kernels for 0% -> 28%
where the time goes in v1:
time: 729 us; the launch traced here: 720 us
  waiting for transfers between devices  279 us (38%)
  Pallas kernels  199 us (27%)
  matrix products  95.4 us (13%)
  local copies, waits for them, and re-layouts  70.6 us (10%)
  other arithmetic  51.1 us (7%)
  between operations  15.3 us (2%)
  starting transfers between devices  9.87 us (1%)
    pallas_call x2, Pallas kernels, sum_over_group(): pl.pallas_call(sum_kernel, out_shape=[jax.ShapeDtypeStruct(array.shape, a...  199 us
    all_gather x4, waiting for transfers between devices, spread_rows(): return lax.all_gather(shard, 'tensor', axis=0, tiled=True)  78.8 us
    reduce_scatter x4, waiting for transfers between devices, sum_backward(): lax.psum_scatter(partial_value(jnp.int32(0), my_rows * lax.axis_size('ten...  71.6 us
    reduce_scatter x2, waiting for transfers between devices, sum_forward(): lax.psum_scatter(partial_value(jnp.int32(0), my_rows * lax.axis_size('ten...  56.5 us
    all_gather x4, waiting for transfers between devices, spread_grads(): return lax.all_gather(shard, 'tensor', axis=0, tiled=True)  55.9 us
    unnamed x108, local copies, waits for them, and re-layouts  14.7 us
  transfers between devices with their start and end apart: 18, of which 15 were waited for; matrix products, arithmetic and copies ran while one was open for 14% of the time, Pallas kernels for 28%

profile of v1, /device:TPU:0, one launch (start us, length us, event | category | flops | bytes accessed | tf_op | source)
XLA Modules:
  0.0 719.5 jit_solution(1132960002471808572)
XLA Ops:
  11.8 20.2 %all-gather.13.cloned.1.call-done = bf16[1024,768]{1,0:T(8,128)(2,1)} async-done(((bf16[256,768]{1,0:T(8,128)(2,1)}), bf16[1024,768]{1,0:T(8,128)(2,1)}) %all-gather.13.cloned.1.call-update) | async-done | bytes 1572880 | tf_op jit(solution)/shard_map/all_gather | solution.py:340
  32.0 2.8 fusion.22
  45.9 4.2 all-to-all-start
  51.6 6.0 all-to-all-done
  61.6 19.8 %all-gather.15.cloned.1.call-done = bf16[1024,768]{1,0:T(8,128)(2,1)} async-done(((bf16[256,768]{1,0:T(8,128)(2,1)}), bf16[1024,768]{1,0:T(8,128)(2,1)}) %all-gather.15.cloned.1.call-update) | async-done | bytes 1572880 | tf_op jit(solution)/shard_map/all_gather | solution.py:340
  81.5 3.3 fusion.54
  86.4 3.2 convolution_convert_fusion.5
  89.8 28.2 %reduce-scatter.7.cloned.1.call-done = bf16[256,768]{1,0:T(8,128)(2,1)} async-done(((bf16[1024,768]{1,0:T(8,128)(2,1)}), bf16[256,768]{1,0:T(8,128)(2,1)}) %reduce-scatter.7.cloned.1.call-update) | async-done | bytes 393232 | tf_op jit(solution)/shard_map/reduce_scatter | solution.py:308
  122.2 19.1 %all-gather.17.cloned.1.call-done = bf16[1024,768]{1,0:T(8,128)(2,1)} async-done(((bf16[256,768]{1,0:T(8,128)(2,1)}), bf16[1024,768]{1,0:T(8,128)(2,1)}) %all-gather.17.cloned.1.call-update) | async-done | bytes 1572880 | tf_op jit(solution)/shard_map/all_gather | solution.py:340
  141.3 2.7 fusion.18
  148.3 2.7 fusion.121
  160.5 4.1 all-to-all-start.1
  164.7 7.4 %all-to-all-done.1 = bf16[4,256,192]{1,2,0:T(8,128)(2,1)} async-done(((bf16[4,256,192]{1,2,0:T(8,128)(2,1)}), bf16[4,256,192]{1,2,0:T(8,128)(2,1)}, u32[]{:S(2)}, u32[]{:S(2)}) %all-to-all-start.1) | async-done | bytes 393248 | tf_op jit(solution)/shard_map/all_to_all | solution.py:331
  176.3 19.8 %all-gather.19.cloned.1.call-done = bf16[1024,768]{1,0:T(8,128)(2,1)} async-done(((bf16[256,768]{1,0:T(8,128)(2,1)}), bf16[1024,768]{1,0:T(8,128)(2,1)}) %all-gather.19.cloned.1.call-update) | async-done | bytes 1572880 | tf_op jit(solution)/shard_map/all_gather | solution.py:340
  196.0 3.3 fusion.45
  201.0 3.2 convolution_convert_fusion.4
  204.3 28.2 %reduce-scatter.9.cloned.1.call-done = bf16[256,768]{1,0:T(8,128)(2,1)} async-done(((bf16[1024,768]{1,0:T(8,128)(2,1)}), bf16[256,768]{1,0:T(8,128)(2,1)}) %reduce-scatter.9.cloned.1.call-update) | async-done | bytes 393232 | tf_op jit(solution)/shard_map/reduce_scatter | solution.py:308
  237.9 19.3 %all-gather.21.cloned.1.call-done = bf16[1024,768]{1,0:T(8,128)(2,1)} async-done(((bf16[256,768]{1,0:T(8,128)(2,1)}), bf16[1024,768]{1,0:T(8,128)(2,1)}) %all-gather.21.cloned.1.call-update) | async-done | bytes 1572880 | tf_op jit(solution)/shard_map/all_gather | solution.py:344
  257.2 5.9 convert_reduce_fusion
  264.3 2.6 convolution_convert_fusion.3
  266.9 28.3 %reduce-scatter.11.cloned.1.call-done = bf16[256,768]{1,0:T(8,128)(2,1)} async-done(((bf16[1024,768]{1,0:T(8,128)(2,1)}), bf16[256,768]{1,0:T(8,128)(2,1)}) %reduce-scatter.11.cloned.1.call-update) | async-done | bytes 393232 | tf_op jit(solution)/shard_map/reduce_scatter | solution.py:322
  297.1 2.8 fusion.116
  300.0 2.8 fusion.123
  302.8 17.0 %all-gather.23.cloned.1.call-done = bf16[1024,768]{1,0:T(8,128)(2,1)} async-done(((bf16[256,768]{1,0:T(8,128)(2,1)}), bf16[1024,768]{1,0:T(8,128)(2,1)}) %all-gather.23.cloned.1.call-update) | async-done | bytes 1572880 | tf_op jit(solution)/shard_map/all_gather | solution.py:344
  319.8 2.9 convolution_convert_fusion.13
  324.7 3.1 fusion.33
  346.4 3.7 convolution_convert_fusion.1
  350.2 28.3 %reduce-scatter.13.cloned.1.call-done = bf16[256,768]{1,0:T(8,128)(2,1)} async-done(((bf16[1024,768]{1,0:T(8,128)(2,1)}), bf16[256,768]{1,0:T(8,128)(2,1)}) %reduce-scatter.13.cloned.1.call-update) | async-done | bytes 393232 | tf_op jit(solution)/shard_map/reduce_scatter | solution.py:322
  380.4 2.8 fusion.115
  383.5 19.6 %all-gather.25.cloned.1.call-done = bf16[1024,768]{1,0:T(8,128)(2,1)} async-done(((bf16[256,768]{1,0:T(8,128)(2,1)}), bf16[1024,768]{1,0:T(8,128)(2,1)}) %all-gather.25.cloned.1.call-update) | async-done | bytes 1572880 | tf_op jit(solution)/shard_map/all_gather | solution.py:344
  403.1 5.9 convert_reduce_fusion.3
  410.2 2.6 convolution_convert_fusion.2
  417.6 2.6 convolution_convert_fusion.6.up
  420.2 3.0 convolution_convert_fusion.7.down
  426.1 15.0 %reduce-scatter.15.cloned.1.call-done = bf16[256,768]{1,0:T(8,128)(2,1)} async-done(((bf16[1024,768]{1,0:T(8,128)(2,1)}), bf16[256,768]{1,0:T(8,128)(2,1)}) %reduce-scatter.15.cloned.1.call-update) | async-done | bytes 393232 | tf_op jit(solution)/shard_map/reduce_scatter | solution.py:322
  443.0 2.8 fusion.114
  445.9 2.5 convert_element_type.496
  451.9 2.8 convolution_convert_fusion.16.out
  454.7 99.0 %shard_map.221 = (f32[16,768]{1,0:T(8,128)}, bf16[768,768]{1,0:T(8,128)(2,1)}, bf16[768,768]{1,0:T(8,128)(2,1)}, bf16[768,576]{1,0:T(8,128)(2,1)}, bf16[192,768]{1,0:T(8,128)(2,1)}) custom-call(f32[16,768]{1,0:T(8,128)} %concatenate.7.small, bf16[768,768]{1,0:T(8,128)(2,1)} %convolution_convert_fusion.7.down, bf16[768,768]{1,0:T(8,128)(2,1)} %convolution_convert_fusion.6.up, ...), custom_call_target="tpu_custom_call" | custom-call | tf_op jit(solution)/shard_map/pallas_call | solution.py:254
  553.8 2.5 copy.80
  560.3 4.5 convolution_convert_fusion.8.up
  564.8 3.0 convolution_convert_fusion.9.down
  567.8 2.8 convolution_convert_fusion.11
  581.0 3.9 convolution_convert_fusion
  585.2 4.1 fusion.24
  594.3 99.5 %shard_map.220 = (f32[16,768]{1,0:T(8,128)}, bf16[768,768]{1,0:T(8,128)(2,1)}, bf16[768,768]{1,0:T(8,128)(2,1)}, bf16[768,576]{1,0:T(8,128)(2,1)}, bf16[192,768]{1,0:T(8,128)(2,1)}) custom-call(f32[16,768]{1,0:T(8,128)} %concatenate.6.small, bf16[768,768]{1,0:T(8,128)(2,1)} %convolution_convert_fusion.9.down, bf16[768,768]{1,0:T(8,128)(2,1)} %convolution_convert_fusion.8.up, ...), custom_call_target="tpu_custom_call" | custom-call | tf_op jit(solution)/shard_map/pallas_call | solution.py:254
  705.6 2.5 maximum_convert_fusion
  708.1 2.5 maximum_convert_fusion.1
  (283 shorter events, 125.5 us)
Async XLA Ops:
  7.2 24.8 %all-gather.13.cloned.1.call-start = ((), (), s32[]{:S(2)}) async-start(), calls=%async_computation.8 | async-start | bytes 1966080 | tf_op jit(solution)/shard_map/all_gather | solution.py:340
  7.9 43.7 %all-gather.29.cloned.1.call-start = ((), (), s32[]{:S(2)}) async-start(), calls=%async_computation.22 | async-start | bytes 1474560 | tf_op jit(solution)/shard_map/all_gather | solution.py:334
  41.2 3.0 copy-start.14
  44.1 6.1 copy-start.36
  44.1 6.1 copy-start.34
  44.1 6.1 copy-start.35
  45.9 15.7 %copy-start.37 = (bf16[2,768]{1,0:T(2,128)(2,1)S(1)}, bf16[2,768]{1,0:T(2,128)(2,1)}, u32[]{:S(2)}) copy-start(bf16[2,768]{1,0:T(2,128)(2,1)} %param.23) | copy-start | bytes 9220
  45.9 11.7 %all-to-all-start = ((bf16[4,256,192]{1,2,0:T(8,128)(2,1)}), bf16[4,256,192]{1,2,0:T(8,128)(2,1)}, u32[]{:S(2)}, u32[]{:S(2)}) async-start(bf16[4,256,192]{1,2,0:T(8,128)(2,1)} %bitcast.197), calls=%async_computation | async-start | bytes 786432 | tf_op jit(solution)/shard_map/all_to_all | solution.py:331
  50.1 31.4 %all-gather.15.cloned.1.call-start = ((), (), s32[]{:S(2)}) async-start(), calls=%async_computation.9 | async-start | bytes 1966080 | tf_op jit(solution)/shard_map/all_gather | solution.py:340
  61.5 56.5 %reduce-scatter.7.cloned.1.call-start = ((), (), s32[]{:S(2)}) async-start(), calls=%async_computation.10 | async-start | bytes 1966080 | tf_op jit(solution)/shard_map/reduce_scatter | solution.py:308
  81.5 5.0 copy-start.39
  86.4 3.3 copy-start.38
  89.7 51.6 %all-gather.17.cloned.1.call-start = ((), (), s32[]{:S(2)}) async-start(), calls=%async_computation.11 | async-start | bytes 1966080 | tf_op jit(solution)/shard_map/all_gather | solution.py:340
  121.5 43.2 %all-gather.31.cloned.1.call-start = ((), (), s32[]{:S(2)}) async-start(), calls=%async_computation.23 | async-start | bytes 1474560 | tf_op jit(solution)/shard_map/all_gather | solution.py:334
  155.8 2.9 copy-start.16
  160.5 11.6 %all-to-all-start.1 = ((bf16[4,256,192]{1,2,0:T(8,128)(2,1)}), bf16[4,256,192]{1,2,0:T(8,128)(2,1)}, u32[]{:S(2)}, u32[]{:S(2)}) async-start(bf16[4,256,192]{1,2,0:T(8,128)(2,1)} %bitcast.199), calls=%async_computation.2 | async-start | bytes 786432 | tf_op jit(solution)/shard_map/all_to_all | solution.py:331
  164.6 31.4 %all-gather.19.cloned.1.call-start = ((), (), s32[]{:S(2)}) async-start(), calls=%async_computation.12 | async-start | bytes 1966080 | tf_op jit(solution)/shard_map/all_gather | solution.py:340
  176.2 56.3 %reduce-scatter.9.cloned.1.call-start = ((), (), s32[]{:S(2)}) async-start(), calls=%async_computation.13 | async-start | bytes 1966080 | tf_op jit(solution)/shard_map/reduce_scatter | solution.py:308
  196.0 5.0 copy-start.40
  204.3 53.0 %all-gather.21.cloned.1.call-start = ((), (), s32[]{:S(2)}) async-start(), calls=%async_computation.14 | async-start | bytes 1966080 | tf_op jit(solution)/shard_map/all_gather | solution.py:344
  232.6 3.3 copy-start.26
  237.4 57.8 %reduce-scatter.11.cloned.1.call-start = ((), (), s32[]{:S(2)}) async-start(), calls=%async_computation.15 | async-start | bytes 1966080 | tf_op jit(solution)/shard_map/reduce_scatter | solution.py:322
  257.2 7.1 copy-start.41
  266.9 52.9 %all-gather.23.cloned.1.call-start = ((), (), s32[]{:S(2)}) async-start(), calls=%async_computation.16 | async-start | bytes 1966080 | tf_op jit(solution)/shard_map/all_gather | solution.py:344
  300.0 78.5 %reduce-scatter.13.cloned.1.call-start = ((), (), s32[]{:S(2)}) async-start(), calls=%async_computation.17 | async-start | bytes 1966080 | tf_op jit(solution)/shard_map/reduce_scatter | solution.py:322
  324.7 3.1 copy-start.1
  324.7 3.1 copy-start.17
  324.7 3.2 copy-start.21
  350.2 52.9 %all-gather.25.cloned.1.call-start = ((), (), s32[]{:S(2)}) async-start(), calls=%async_computation.18 | async-start | bytes 1966080 | tf_op jit(solution)/shard_map/all_gather | solution.py:344
  383.2 57.9 %reduce-scatter.15.cloned.1.call-start = ((), (), s32[]{:S(2)}) async-start(), calls=%async_computation.19 | async-start | bytes 1966080 | tf_op jit(solution)/shard_map/reduce_scatter | solution.py:322
  403.1 7.1 copy-start.42
  412.7 155.1 %all-gather.27.cloned.1.call-start = ((), (), s32[]{:S(2)}) async-start(), calls=%async_computation.20 | async-start | bytes 1966080 | tf_op jit(solution)/shard_map/all_gather | solution.py:344
  412.8 4.4 copy-start.23
  412.8 4.7 copy-start.44
  412.8 4.7 copy-start.50
  420.2 3.0 copy-start.11
  420.2 3.1 copy-start.12
  420.2 3.3 copy-start.7
  420.2 3.6 copy-start.32
  420.2 3.6 copy-start.43
  445.8 264.8 %reduce-scatter.17.cloned.1.call-start = ((), (), s32[]{:S(2)}) async-start(), calls=%async_computation.21 | async-start | bytes 1966080 | tf_op jit(solution)/shard_map/reduce_scatter | solution.py:322
  560.3 4.5 copy-start.24
  560.3 4.5 copy-start.46
  581.0 3.9 copy-start.8
  585.2 7.9 %copy-start.25 = (bf16[24,8,4,256]{3,1,2,0:T(8,128)(2,1)S(1)}, bf16[24,8,4,256]{3,1,2,0:T(8,128)(2,1)}, u32[]{:S(2)}) copy-start(bf16[24,8,4,256]{3,1,2,0:T(8,128)(2,1)} %copy.89) | copy-start | bytes 1179652
  594.3 109.3 %copy-start.13 = (bf16[768,576]{0,1:T(8,128)(2,1)S(1)}, bf16[768,576]{0,1:T(8,128)(2,1)}, u32[]{:S(2)}) copy-start(bf16[768,576]{0,1:T(8,128)(2,1)} %copy.80) | copy-start | bytes 2654212
  701.2 4.3 copy-start.28
  701.2 4.3 copy-start.30
  (22 other events, 36.5 us)
Sparse Core Ops, SparseCore 0:
  9.6 22.3 all-gather.12
  34.1 17.4 all-gather.28
  61.7 19.7 all-gather.14
  89.8 28.1 reduce-scatter.6
  121.6 19.6 all-gather.16
  142.8 17.4 all-gather.30
  176.3 19.6 all-gather.18
  204.4 28.1 reduce-scatter.8
  237.5 19.6 all-gather.20
  267.0 28.1 reduce-scatter.10
  300.1 19.6 all-gather.22
  350.3 28.1 reduce-scatter.12
  383.4 19.6 all-gather.24
  412.9 28.1 reduce-scatter.14
  445.9 20.1 all-gather.26
  585.0 28.4 reduce-scatter.16

commit v2 on v1

--- a/solution.py
+++ b/solution.py
@@ -6,6 +6,13 @@
 from jax.sharding import PartitionSpec as P
 
 HEAD = 64
+norm_eps = 1e-05
+
+
+def gelu_tanh(pre_active):
+    return jax.nn.gelu(pre_active, approximate=True)
+
+
 MESH = pl.DeviceIdType.MESH
 Y_SIZE = 2
 Z_SIZE = 4
@@ -28,6 +35,7 @@
         self.is_inner = jnp.logical_not(self.is_end)
         self.core = (self.dp, self.t + 1 - 2 * lax.rem(self.t, 2))
         self.over = (self.dp, lax.rem(self.t + 2, 4))
+        self.diagonal = (self.dp, 3 - self.t)
         self.y_pair = (base + self.z * Y_SIZE + 1 - self.y, self.t)
         self.z_pair = (base + z_pair * Y_SIZE + self.y, self.t)
         self.z_mid = (base + z_mid * Y_SIZE + self.y, self.t)
@@ -271,11 +279,372 @@
     return [lax.psum(value, "dp", axis_index_groups=groups) for value in values]
 
 
-norm_eps = 1e-05
-
-
-def gelu_tanh(pre_active):
-    return jax.nn.gelu(pre_active, approximate=True)
+CORNER = 128
+LANES = 128
+SLOT = 256
+
+
+def product(left, right, contract):
+    return lax.dot_general(left, right, ((contract[:1], contract[1:]), ((), ())), preferred_element_type=F32)
+
+
+def nn(left, right):
+    return product(left, right, (1, 0))
+
+
+def nt(left, right):
+    return product(left, right, (1, 1))
+
+
+def tn(left, right):
+    return product(left, right, (0, 0))
+
+
+class Gather:
+    def __init__(self, place, links, rows):
+        half = SLOT // 2
+        self.near_copies, self.far_copies, self.pass_copies = [], [], []
+        for part in range(2):
+            own = pl.ds(part * half, half)
+            beside = pl.ds(SLOT + part * half, half)
+            over = pl.ds(2 * SLOT + part * half, half)
+            diagonal = pl.ds(3 * SLOT + part * half, half)
+            self.near_copies.append(links.copy(rows.at[own], rows.at[beside], place.core))
+            self.far_copies.append(links.copy(rows.at[own], rows.at[over], place.over))
+            self.pass_copies.append(links.copy(rows.at[over], rows.at[diagonal], place.core))
+
+    def send(self, part):
+        self.far_copies[part].start()
+        self.near_copies[part].start()
+
+    def near(self):
+        for copy in self.near_copies:
+            copy.wait_recv()
+
+    def far(self, part):
+        self.far_copies[part].wait_recv()
+        self.pass_copies[part].start()
+
+    def diagonal(self, part):
+        self.pass_copies[part].wait_recv()
+
+    def drain(self):
+        for copy in self.near_copies + self.far_copies + self.pass_copies:
+            copy.wait_send()
+
+
+class Scatter:
+    def __init__(self, place, links, rooms):
+        self.core_out, self.core_in, self.far_out, self.far_in, self.near_out, self.near_in = rooms
+        self.core_copies = [
+            links.copy(self.core_out.at[part], self.core_in.at[part], place.core) for part in range(2)
+        ]
+        self.far_copies = [
+            links.copy(self.far_out.at[part], self.far_in.at[part], place.over) for part in range(2)
+        ]
+        self.near_copies = [
+            links.copy(self.near_out.at[part], self.near_in.at[part], place.core) for part in range(2)
+        ]
+
+    def beside(self, term):
+        half = SLOT // 2
+        for part in range(2):
+            self.near_out[part] = term[part * half : (part + 1) * half].astype(BF16)
+            self.near_copies[part].start()
+
+    def diagonal(self, part, term):
+        self.core_out[part] = term.astype(BF16)
+        self.core_copies[part].start()
+
+    def over(self, part, term):
+        self.core_copies[part].wait_recv()
+        self.far_out[part] = (term + self.core_in[part].astype(F32)).astype(BF16)
+        self.far_copies[part].start()
+
+    def arrived(self, part):
+        self.near_copies[part].wait_recv()
+        self.far_copies[part].wait_recv()
+        return self.near_in[part].astype(F32) + self.far_in[part].astype(F32)
+
+    def drain(self):
+        for copy in self.core_copies + self.far_copies + self.near_copies:
+            copy.wait_send()
+
+
+def lane_masks():
+    lane = lax.broadcasted_iota(jnp.int32, (1, LANES), 1)
+    first = jnp.where(lane < HEAD, 1.0, 0.0).astype(BF16)
+    return first, (1.0 - first.astype(F32)).astype(BF16)
+
+
+def head_parts(tile, masks):
+    parts = []
+    width = tile.shape[-1]
+    for first in range(0, width, LANES):
+        piece = tile[:, first : min(first + LANES, width)]
+        if piece.shape[-1] == HEAD:
+            parts.append([piece])
+        else:
+            parts.append([piece * masks[0], piece * masks[1]])
+    return parts
+
+
+def whole_parts(tile):
+    width = tile.shape[-1]
+    return [tile[:, first : min(first + LANES, width)] for first in range(0, width, LANES)]
+
+
+def allowed_rows(seg_cols, seg_rows, slot):
+    return seg_cols[:, slot : slot + 1] == seg_rows[slot : slot + 1, :]
+
+
+def attention_forward(query, keys, values, allowed):
+    masks = lane_masks()
+    outs = []
+    for query_part, key_heads, value_heads in zip(
+        whole_parts(query), head_parts(keys, masks), head_parts(values, masks)
+    ):
+        total = None
+        for key_head, value_head in zip(key_heads, value_heads):
+            scores = jnp.where(allowed, nt(query_part, key_head), -1000000000.0)
+            grown = jnp.exp(scores - jnp.max(scores, axis=-1, keepdims=True))
+            probs = grown * (1.0 / jnp.sum(grown, axis=-1, keepdims=True))
+            term = nn(probs.astype(BF16), value_head)
+            total = term if total is None else total + term
+        outs.append(total.astype(BF16))
+    return outs
+
+
+def norm_rows(total, gain, shift):
+    average = jnp.mean(total, axis=-1, keepdims=True)
+    centered = total - average
+    inverse = lax.rsqrt(jnp.mean(centered * centered, axis=-1, keepdims=True) + norm_eps)
+    scaled = centered * inverse
+    return scaled * gain + shift, scaled, inverse
+
+
+OUT_BIAS, DOWN_BIAS, UP_BIAS, Q_BIAS, V_BIAS, GAIN, SHIFT = 0, 1, 2, 3, 4, 5, 7
+
+
+def forward_kernel(
+    hidden, seg_rows, seg_cols, small, qkv_all, out_all, up_all, down_all,
+    result, full_in, query, keys, values, context, full_mid, pre, active, scaled, inverse,
+    qkv_weight, out_weight, up_weight, down_weight, context_in, own_part, far_part, state,
+    core_out, core_in, far_out, far_in, near_out, near_in, load_sems, sems,
+):
+    place = Place()
+    links = Links(sems)
+    layers = qkv_weight.shape[0]
+    local = query.shape[-1]
+    half = SLOT // 2
+    halves = [pl.ds(part * half, half) for part in range(2)]
+    slots = [pl.ds(slot * SLOT, SLOT) for slot in range(4)]
+    loads = []
+    for layer in range(layers):
+        row = []
+        for at, (source, target) in enumerate(
+            (
+                (qkv_all.at[layer], qkv_weight.at[layer]),
+                (out_all.at[layer], out_weight.at[layer, 0]),
+                (up_all.at[layer], up_weight.at[layer]),
+                (down_all.at[layer], down_weight.at[layer]),
+            )
+        ):
+            copy = pltpu.make_async_copy(source, target, load_sems.at[layer, at])
+            copy.start()
+            row.append(copy)
+        loads.append(row)
+    greet((place.core, place.over, place.diagonal))
+    rooms = (core_out, core_in, far_out, far_in, near_out, near_in)
+
+    state[...] = hidden[...].astype(F32)
+    gather = Gather(place, links, full_in.at[0])
+    for part in range(2):
+        full_in[0, halves[part]] = hidden[halves[part]]
+        gather.send(part)
+    drains = []
+    for layer in range(layers):
+        vector = lambda row, width=small.shape[-1]: small[layer, row : row + 1, :width]
+
+        def attend(slot):
+            rows = slots[slot]
+            mixed = nn(full_in[layer, rows], qkv_weight[layer])
+            query[layer, rows] = (
+                (mixed[:, :local] + vector(Q_BIAS, local)) * HEAD ** (-0.5)
+            ).astype(BF16)
+            keys[layer, rows] = mixed[:, SLOT : SLOT + local].astype(BF16)
+            values[layer, rows] = (mixed[:, 2 * SLOT : 2 * SLOT + local] + vector(V_BIAS, local)).astype(BF16)
+            outs = attention_forward(
+                query[layer, rows], keys[layer, rows], values[layer, rows],
+                allowed_rows(seg_cols, seg_rows, slot),
+            )
+            first = 0
+            for out in outs:
+                context[layer, rows, first : first + out.shape[-1]] = out
+                first += out.shape[-1]
+
+        sends = [
+            links.copy(context.at[layer, slots[slot]], context_in.at[slot], device)
+            for slot, device in ((1, place.core), (2, place.over), (3, place.diagonal))
+        ]
+        out_near = links.copy(out_weight.at[layer, 0], out_weight.at[layer, 1], place.core)
+        out_far = links.copy(out_weight.at[layer, 0], out_weight.at[layer, 2], place.over)
+        out_pass = links.copy(out_weight.at[layer, 2], out_weight.at[layer, 3], place.core)
+        loads[layer][1].wait()
+        out_near.start()
+        loads[layer][0].wait()
+        attend(0)
+        gather.near()
+        attend(1)
+        sends[0].start()
+        gather.far(0)
+        gather.far(1)
+        out_far.start()
+        gather.diagonal(0)
+        gather.diagonal(1)
+        attend(2)
+        sends[1].start()
+        out_far.wait_recv()
+        out_pass.start()
+        attend(3)
+        sends[2].start()
+        own_part[...] = nn(context[layer, slots[0]], out_weight[layer, 0])
+        out_near.wait_recv()
+        sends[0].wait_recv()
+        own_part[...] += nn(context_in[1], out_weight[layer, 1])
+        out_pass.wait_recv()
+        sends[1].wait_recv()
+        sends[2].wait_recv()
+        gather.drain()
+        gather = Gather(place, links, full_mid.at[layer])
+        for part in range(2):
+            rows = halves[part]
+            total = (
+                own_part[rows]
+                + nn(context_in[2, rows], out_weight[layer, 2])
+                + nn(context_in[3, rows], out_weight[layer, 3])
+                + state[rows]
+                + vector(OUT_BIAS)
+            )
+            normed, scaled_part, inverse_part = norm_rows(total, vector(GAIN), vector(SHIFT))
+            full_mid[layer, rows] = normed.astype(BF16)
+            gather.send(part)
+            state[rows] = normed
+            scaled[layer, 0, rows] = scaled_part
+            inverse[layer, 0, rows] = jnp.broadcast_to(inverse_part, (half, LANES))
+        for copy in sends + [out_near, out_far, out_pass]:
+            drains.append(copy)
+        loads[layer][2].wait()
+        loads[layer][3].wait()
+        scatter = Scatter(place, links, rooms)
+
+        def feed(pieces):
+            for first in range(0, up_weight.shape[-1], SLOT):
+                columns = slice(first, first + SLOT)
+                rows_in = jnp.concatenate([full_mid[layer, piece] for piece in pieces])
+                raised = nn(rows_in, up_weight[layer, :, columns]) + small[layer, UP_BIAS : UP_BIAS + 1, columns]
+                shaped = gelu_tanh(raised).astype(BF16)
+                size = rows_in.shape[0] // len(pieces)
+                for at, piece in enumerate(pieces):
+                    pre[layer, piece, columns] = raised[at * size : (at + 1) * size]
+                    active[layer, piece, columns] = shaped[at * size : (at + 1) * size]
+            return nn(jnp.concatenate([active[layer, piece] for piece in pieces]), down_weight[layer])
+
+        own_part[...] = feed([slots[0]])
+        gather.near()
+        scatter.beside(feed([slots[1]]))
+        for part in range(2):
+            gather.far(part)
+            gather.diagonal(part)
+            far_part[...] = feed(
+                [pl.ds(2 * SLOT + part * half, half), pl.ds(3 * SLOT + part * half, half)]
+            )
+            scatter.diagonal(part, far_part[half:])
+            scatter.over(part, far_part[:half])
+        gather.drain()
+        if layer < layers - 1:
+            gather = Gather(place, links, full_in.at[layer + 1])
+        for part in range(2):
+            rows = halves[part]
+            total = state[rows] + own_part[rows] + scatter.arrived(part) + vector(DOWN_BIAS)
+            normed, scaled_part, inverse_part = norm_rows(total, vector(GAIN + 1), vector(SHIFT + 1))
+            state[rows] = normed
+            if layer < layers - 1:
+                full_in[layer + 1, rows] = normed.astype(BF16)
+                gather.send(part)
+            else:
+                result[rows] = normed.astype(BF16)
+            scaled[layer, 1, rows] = scaled_part
+            inverse[layer, 1, rows] = jnp.broadcast_to(inverse_part, (half, LANES))
+        scatter.drain()
+    for copy in drains:
+        copy.wait_send()
+
+
+def run_forward(hidden, seg_rows, seg_cols, small, qkv_all, out_all, up_all, down_all):
+    layers, width, wide = qkv_all.shape
+    local, hidden_units = out_all.shape[1], up_all.shape[-1]
+    rows = hidden.shape[0]
+    group = 4 * rows
+    half = rows // 2
+    vmem = pl.BlockSpec(memory_space=pltpu.VMEM)
+    anywhere = pl.BlockSpec(memory_space=pl.ANY)
+    shape = jax.ShapeDtypeStruct
+    return pl.pallas_call(
+        forward_kernel,
+        out_shape=[
+            shape((rows, width), BF16),
+            shape((layers, group, width), BF16),
+            shape((layers, group, local), BF16),
+            shape((layers, group, local), BF16),
+            shape((layers, group, local), BF16),
+            shape((layers, group, local), BF16),
+            shape((layers, group, width), BF16),
+            shape((layers, group, hidden_units), F32),
+            shape((layers, group, hidden_units), BF16),
+            shape((layers, 2, rows, width), F32),
+            shape((layers, 2, rows, LANES), F32),
+        ],
+        in_specs=[vmem] * 4 + [anywhere] * 4,
+        out_specs=[vmem] * 11,
+        scratch_shapes=[
+            pltpu.VMEM(qkv_all.shape, BF16),
+            pltpu.VMEM((layers, 4) + out_all.shape[1:], BF16),
+            pltpu.VMEM(up_all.shape, BF16),
+            pltpu.VMEM(down_all.shape, BF16),
+            pltpu.VMEM((4, rows, local), BF16),
+            pltpu.VMEM((rows, width), F32),
+            pltpu.VMEM((rows, width), F32),
+            pltpu.VMEM((rows, width), F32),
+        ]
+        + [pltpu.VMEM((2, half, width), BF16)] * 6
+        + [pltpu.SemaphoreType.DMA((layers, 4)), pltpu.SemaphoreType.DMA((2, 64))],
+        compiler_params=pltpu.CompilerParams(
+            collective_id=2, has_side_effects=True, vmem_limit_bytes=60 << 20
+        ),
+    )(hidden, seg_rows, seg_cols, small, qkv_all, out_all, up_all, down_all)
+
+
+def packed_inputs(segment_ids, qkv_weight, qv_bias, out_bias, norm_gain, norm_bias, up_bias, down_bias):
+    own = lax.axis_index("tensor")
+    order = jnp.stack([own, own ^ 1, own ^ 2, own ^ 3])
+    seg_rows = segment_ids[order]
+    layers, width, _, local = qkv_weight.shape
+    padded = jnp.pad(qkv_weight, ((0, 0), (0, 0), (0, 0), (0, SLOT - local)))
+    wide = lambda rows: jnp.pad(rows, ((0, 0), (0, 0), (0, width - rows.shape[-1])))
+    small = jnp.concatenate(
+        [
+            out_bias[:, None],
+            down_bias[:, None],
+            wide(up_bias[:, None]),
+            wide(qv_bias),
+            norm_gain,
+            norm_bias,
+            jnp.zeros((layers, 7, width), BF16),
+        ],
+        axis=1,
+    ).astype(F32)
+    return seg_rows, seg_rows.T, small, padded.reshape(layers, width, 3 * SLOT)
 
 
 def norm_forward(total, norm_gain, norm_shift):
@@ -609,13 +978,28 @@
     layer_count = qkv_weight.shape[0]
     sequences = segment_ids.shape[0]
     allowed = (segment_ids[:, :, None] == segment_ids[:, None, :])[:, None]
-    tokens_now = hidden_in.astype(jnp.float32)
+    seg_rows, seg_cols, small, qkv_wide = packed_inputs(
+        segment_ids, qkv_weight, qv_bias, out_bias, norm_gain, norm_bias, up_bias, down_bias
+    )
+    out_hidden, *kept = run_forward(
+        hidden_in, seg_rows, seg_cols, small, qkv_wide, out_weight, up_weight, down_weight
+    )
+    own = lax.axis_index("tensor")
+    order = jnp.stack([own, own ^ 1, own ^ 2, own ^ 3])
+
+    def sort(kind, layer_index):
+        array = kept[kind][layer_index]
+        return array.reshape((4, -1) + array.shape[1:])[order].reshape(array.shape)
+
     stored_all = []
     for layer_index in range(layer_count):
-        weights = tuple((member[layer_index] for member in params))
-        tokens_now, stored = layer_forward(tokens_now, sequences, allowed, weights)
-        stored_all.append(stored)
-    out_hidden = tokens_now.astype(jnp.bfloat16)
+        query = sort(1, layer_index) * jnp.bfloat16(8)
+        keys = sort(2, layer_index)
+        raw = jnp.where(allowed, jnp.einsum("sqhe,skhe->shqk", head_split(query, sequences), head_split(keys, sequences), preferred_element_type=F32) * 0.125, -1e9)
+        log_total = jax.scipy.special.logsumexp(raw, axis=-1, keepdims=True)
+        stored_all.append((sort(0, layer_index), query, keys, sort(3, layer_index), log_total, sort(4, layer_index),
+          kept[8][layer_index, 0], kept[9][layer_index, 0][:, :1], sort(5, layer_index), sort(6, layer_index), sort(7, layer_index),
+          kept[8][layer_index, 1], kept[9][layer_index, 1][:, :1]))
     gradient = out_cotangent.astype(jnp.float32)
     per_layer = [None] * layer_count
     for layer_index in reversed(range(layer_count)):

time: 729 us -> 645 us (0.88)
  waiting for transfers between devices: 279 us -> 68.3 us
  Pallas kernels: 199 us -> 299 us
  local copies, waits for them, and re-layouts: 70.6 us -> 132 us
  matrix products: 95.4 us -> 75 us
  starting transfers between devices: 9.87 us -> 0.91 us
  other arithmetic: 51.1 us -> 42.5 us
    pallas_call x0 -> x1, Pallas kernels: none -> 99.3 us  [run_forward(): pl.pallas_call(forward_kernel, out_shape=[shape((rows, width), BF16), sha...]
    all_gather x6 -> x0, waiting for transfers between devices: 80.1 us -> none  [the longest x4 78.8 us: spread_rows(): return lax.all_gather(shard, 'tensor', axis=0, tiled=True)]
    reduce_scatter x2 -> x0, waiting for transfers between devices: 56.5 us -> none  [sum_forward(): lax.psum_scatter(partial_value(jnp.int32(0), my_rows * lax.axis_size('ten...]
    gather x0 -> x22, local copies, waits for them, and re-layouts: none -> 51 us  [the longest x20 48.9 us: sort(): return array.reshape((4, -1) + array.shape[1:])[order].reshape(array.shape)]
    reduce_scatter x4, waiting for transfers between devices: 71.6 us -> 39.6 us  [sum_backward(): lax.psum_scatter(partial_value(jnp.int32(0), my_rows * lax.axis_size('ten...]
    all_gather x4, waiting for transfers between devices: 55.9 us -> 28.6 us  [spread_grads(): return lax.all_gather(shard, 'tensor', axis=0, tiled=True)]
    dot_general x10 -> x0, matrix products: 26.3 us -> none  [the longest x2 6.57 us: layer_forward(): jnp.dot(full_mid, up_weight, preferred_element_type=jnp.float32) + up_bias]
    slice x4 -> x10, local copies, waits for them, and re-layouts: 5.14 us -> 20.6 us  [the longest x6 19.1 us: sort(): array = kept[kind][layer_index]]
  transfers between devices with their start and end apart: 18 -> 8, of which waited for: 15 -> 5; matrix products, arithmetic and copies ran while one was open for 14% -> 21% of each run, Pallas kernels for 28% -> 32%
where the time goes in v2:
time: 645 us; the launch traced here: 633 us
  Pallas kernels  299 us (46%)
  local copies, waits for them, and re-layouts  132 us (20%)
  matrix products  75 us (12%)
  waiting for transfers between devices  68.3 us (11%)
  other arithmetic  42.5 us (7%)
  between operations  15.1 us (2%)
    pallas_call x2, Pallas kernels, sum_over_group(): pl.pallas_call(sum_kernel, out_shape=[jax.ShapeDtypeStruct(array.shape, a...  200 us
    pallas_call x1, Pallas kernels, run_forward(): pl.pallas_call(forward_kernel, out_shape=[shape((rows, width), BF16), sha...  99.3 us
    gather x20, local copies, waits for them, and re-layouts, sort(): return array.reshape((4, -1) + array.shape[1:])[order].reshape(array.shape)  48.9 us
    reduce_scatter x4, waiting for transfers between devices, sum_backward(): lax.psum_scatter(partial_value(jnp.int32(0), my_rows * lax.axis_size('ten...  39.6 us
    all_gather x4, waiting for transfers between devices, spread_grads(): return lax.all_gather(shard, 'tensor', axis=0, tiled=True)  28.6 us
    slice x6, local copies, waits for them, and re-layouts, sort(): array = kept[kind][layer_index]  19.1 us
    dot_general x4, matrix products, partial_value(): jnp.einsum('nf,df->nd', full, weight, preferred_element_type=jnp.float32)  13.1 us
  transfers between devices with their start and end apart: 8, of which 5 were waited for; matrix products, arithmetic and copies ran while one was open for 21% of the time, Pallas kernels for 32%

profile of v2, /device:TPU:0, one launch (start us, length us, event | category | flops | bytes accessed | tf_op | source)
XLA Modules:
  0.0 633.3 jit_solution(12718407430018443110)
XLA Ops:
  17.4 2.4 copy.111.qkv_all
  19.9 99.3 %shard_map.220 = (bf16[256,768]{1,0:T(8,128)(2,1)}, bf16[2,1024,768]{2,1,0:T(8,128)(2,1)}, bf16[2,1024,192]{2,1,0:T(8,128)(2,1)}, bf16[2,1024,192]{2,1,0:T(8,128...) custom-call(bf16[256,768]{1,0:T(8,128)(2,1)} %hidden.1, ...), custom_call_target="tpu_custom_call" | custom-call | tf_op jit(solution)/shard_map/pallas_call | solution.py:593
  123.2 2.4 fusion.111
  125.7 4.9 fusion.113
  130.6 2.4 gather_fusion.1
  133.0 14.4 %all-gather.5.cloned.1.call-done = bf16[1024,768]{1,0:T(8,128)(2,1)} async-done(((bf16[256,768]{1,0:T(8,128)(2,1)}), bf16[1024,768]{1,0:T(8,128)(2,1)}) %all-gather.5.cloned.1.call-update) | async-done | bytes 1572880 | tf_op jit(solution)/shard_map/all_gather | solution.py:713
  147.4 6.3 convert_reduce_fusion
  154.8 2.6 convolution_convert_fusion.3
  157.5 2.5 fusion.119
  164.6 2.5 gather_fusion.6
  169.2 2.4 gather_fusion.4
  173.7 12.0 %reduce-scatter.5.cloned.1.call-done = bf16[256,768]{1,0:T(8,128)(2,1)} async-done(((bf16[1024,768]{1,0:T(8,128)(2,1)}), bf16[256,768]{1,0:T(8,128)(2,1)}) %reduce-scatter.5.cloned.1.call-update) | async-done | bytes 393232 | tf_op jit(solution)/shard_map/reduce_scatter | solution.py:691
  193.9 3.0 fusion.19
  198.3 11.8 %all-gather.7.cloned.1.call-done = bf16[1024,768]{1,0:T(8,128)(2,1)} async-done(((bf16[256,768]{1,0:T(8,128)(2,1)}), bf16[1024,768]{1,0:T(8,128)(2,1)}) %all-gather.7.cloned.1.call-update) | async-done | bytes 1572880 | tf_op jit(solution)/shard_map/all_gather | solution.py:713
  210.1 2.8 convolution_convert_fusion.11
  215.0 5.6 exponential_reduce_fusion
  242.2 4.1 convolution_convert_fusion.1
  247.1 27.6 %reduce-scatter.7.cloned.1.call-done = bf16[256,768]{1,0:T(8,128)(2,1)} async-done(((bf16[1024,768]{1,0:T(8,128)(2,1)}), bf16[256,768]{1,0:T(8,128)(2,1)}) %reduce-scatter.7.cloned.1.call-update) | async-done | bytes 393232 | tf_op jit(solution)/shard_map/reduce_scatter | solution.py:691
  279.7 4.3 gather_fusion.5
  284.0 2.4 gather_fusion.8
  289.8 3.7 fusion.116
  293.5 3.2 gather_fusion.13
  296.7 2.3 all-gather.9.cloned.1.call-done
  299.0 6.4 %convert_reduce_fusion.3 = (f32[768]{0:T(1024)}, bf16[1024,768]{1,0:T(8,128)(2,1)S(1)}) fusion(f32[4,256,768]{2,1,0:T(8,128)} %gather_fusion.5, bf16[1024,768]{1,0:T(8,128)(2,1)} %all-gather.9.cloned.1.call-done, bf16[2,768,768]{2,1,0:T(8,128)(2,1)} %down_all.1), kind=kOutput, calls=%fused_computation.44 | convolution fusion | flops 1225260288 | bytes 7474176 | tf_op jit(solution)/shard_map/nd,fd->nf/dot_general | solution.py:826
  306.6 2.6 convolution_convert_fusion.2
  309.3 5.6 fusion.114
  314.9 3.3 gather_fusion.14
  318.2 3.2 gather_fusion.15
  323.7 2.4 gather_fusion.16
  326.1 3.2 gather_fusion.9
  329.3 3.2 gather_fusion.10
  332.5 3.4 gather_fusion.11
  335.9 2.6 gather_fusion.12
  341.5 4.5 convolution_convert_fusion.4.up
  346.0 2.5 convolution_convert_fusion.5.down
  360.8 2.8 convolution_convert_fusion.12.out
  363.6 100.7 %shard_map.222 = (f32[16,768]{1,0:T(8,128)}, bf16[768,768]{1,0:T(8,128)(2,1)}, bf16[768,768]{1,0:T(8,128)(2,1)}, bf16[768,576]{1,0:T(8,128)(2,1)}, bf16[192,768]{1,0:T(8,128)(2,1)}) custom-call(f32[16,768]{1,0:T(8,128)} %concatenate.30.small, bf16[768,768]{1,0:T(8,128)(2,1)} %convolution_convert_fusion.5.down, ...), custom_call_target="tpu_custom_call" | custom-call | tf_op jit(solution)/shard_map/pallas_call | solution.py:262
  464.3 2.4 copy.137
  469.5 4.5 convolution_convert_fusion.6.up
  473.9 2.5 convolution_convert_fusion.7.down
  476.4 3.0 convolution_convert_fusion.10
  481.4 2.3 multiply_reduce_fusion
  492.8 3.9 convolution_convert_fusion
  498.4 2.9 convolution_convert_fusion.9
  504.3 2.3 convolution_convert_fusion.13.out
  506.6 99.5 %shard_map.221 = (f32[16,768]{1,0:T(8,128)}, bf16[768,768]{1,0:T(8,128)(2,1)}, bf16[768,768]{1,0:T(8,128)(2,1)}, bf16[768,576]{1,0:T(8,128)(2,1)}, bf16[192,768]{1,0:T(8,128)(2,1)}) custom-call(f32[16,768]{1,0:T(8,128)} %concatenate.29.small, bf16[768,768]{1,0:T(8,128)(2,1)} %convolution_convert_fusion.7.down, ...), custom_call_target="tpu_custom_call" | custom-call | tf_op jit(solution)/shard_map/pallas_call | solution.py:262
  618.5 2.5 maximum_convert_fusion
  621.1 2.5 maximum_convert_fusion.1
  (277 shorter events, 118.7 us)
Async XLA Ops:
  7.2 140.3 %all-gather.5.cloned.1.call-start = ((), (), s32[]{:S(2)}) async-start(), calls=%async_computation.4 | async-start | bytes 1966080 | tf_op jit(solution)/shard_map/all_gather | solution.py:713
  7.3 161.9 %copy-start.46 = (s32[1024]{0:T(1024)}, s32[1024]{0:T(1024)S(1)}, u32[]{:S(2)}) copy-start(s32[1024]{0:T(1024)S(1)} %pad_clamp_fusion) | copy-start | bytes 12292
  8.6 11.3 %copy-start.48 = (s32[4,256]{1,0:T(4,128)}, s32[4,256]{1,0:T(4,128)S(1)}, u32[]{:S(2)}) copy-start(s32[4,256]{1,0:T(4,128)S(1)} %gather_fusion) | copy-start | bytes 12292
  19.9 101.3 %copy-start.23 = (bf16[256,768]{1,0:T(8,128)(2,1)S(1)}, bf16[256,768]{1,0:T(8,128)(2,1)}, u32[]{:S(2)}) copy-start(bf16[256,768]{1,0:T(8,128)(2,1)} %param.15) | copy-start | bytes 1179652
  125.6 60.1 %reduce-scatter.5.cloned.1.call-start = ((), (), s32[]{:S(2)}) async-start(), calls=%async_computation.5 | async-start | bytes 1966080 | tf_op jit(solution)/shard_map/reduce_scatter | solution.py:691
  133.0 21.9 %copy-start.13 = (bf16[2,768,768]{2,1,0:T(8,128)(2,1)S(1)}, bf16[2,768,768]{2,1,0:T(8,128)(2,1)}, u32[]{:S(2)}) copy-start(bf16[2,768,768]{2,1,0:T(8,128)(2,1)} %up_all.1) | copy-start | bytes 7077892
  154.8 2.6 copy-start.35
  157.4 52.7 %all-gather.7.cloned.1.call-start = ((), (), s32[]{:S(2)}) async-start(), calls=%async_computation.6 | async-start | bytes 1966080 | tf_op jit(solution)/shard_map/all_gather | solution.py:713
  157.5 4.0 copy-start.34
  163.3 22.4 %copy-start = (f32[2,2,256,768]{3,2,1,0:T(8,128)S(1)}, f32[2,2,256,768]{3,2,1,0:T(8,128)}, u32[]{:S(2)}) copy-start(f32[2,2,256,768]{3,2,1,0:T(8,128)} %get-tuple-element.35) | copy-start | bytes 9437188
  164.6 9.0 %copy-start.39 = (f32[256,128]{1,0:T(8,128)S(1)}, f32[256,128]{1,0:T(8,128)}, u32[]{:S(2)}) copy-start(f32[256,128]{1,0:T(8,128)} %get-tuple-element.106) | copy-start | bytes 393220
  185.8 4.8 copy-start.40
  190.3 84.4 %reduce-scatter.7.cloned.1.call-start = ((), (), s32[]{:S(2)}) async-start(), calls=%async_computation.7 | async-start | bytes 1966080 | tf_op jit(solution)/shard_map/reduce_scatter | solution.py:691
  190.7 3.0 copy-start.15
  193.7 3.1 copy-start.2
  193.8 3.0 copy-start.24
  193.9 3.0 copy-start.5
  215.0 5.6 copy-start.3
  242.2 4.2 copy-start.38
  246.3 52.7 %all-gather.9.cloned.1.call-start = ((), (), s32[]{:S(2)}) async-start(), calls=%async_computation.8 | async-start | bytes 1966080 | tf_op jit(solution)/shard_map/all_gather | solution.py:713
  274.7 5.0 copy-start.47
  279.2 77.5 %reduce-scatter.9.cloned.1.call-start = ((), (), s32[]{:S(2)}) async-start(), calls=%async_computation.9 | async-start | bytes 1966080 | tf_op jit(solution)/shard_map/reduce_scatter | solution.py:691
  279.7 8.9 %copy-start.51 = (f32[768]{0:T(1024)S(1)}, f32[768]{0:T(1024)}, u32[]{:S(2)}) copy-start(f32[768]{0:T(1024)} %get-tuple-element.60) | copy-start | bytes 9220
  279.7 9.5 %copy-start.50 = (f32[768]{0:T(1024)S(1)}, f32[768]{0:T(1024)}, u32[]{:S(2)}) copy-start(f32[768]{0:T(1024)} %get-tuple-element.69) | copy-start | bytes 9220
  299.0 7.6 %copy-start.14 = (bf16[2,768,768]{2,1,0:T(8,128)(2,1)S(1)}, bf16[2,768,768]{2,1,0:T(8,128)(2,1)}, u32[]{:S(2)}) copy-start(bf16[2,768,768]{2,1,0:T(8,128)(2,1)} %up_all.1) | copy-start | bytes 7077892
  309.2 167.2 %all-gather.11.cloned.1.call-start = ((), (), s32[]{:S(2)}) async-start(), calls=%async_computation.10 | async-start | bytes 1966080 | tf_op jit(solution)/shard_map/all_gather | solution.py:713
  332.5 5.9 copy-start.37
  341.5 4.5 copy-start.19
  341.5 4.5 copy-start.28
  346.0 2.8 copy-start.29
  346.0 2.8 copy-start.45
  350.9 4.6 copy-start.57
  350.9 4.6 copy-start.58
  350.9 5.9 copy-start.49
  350.9 7.5 %copy-start.59 = (f32[256]{0:T(256)S(1)}, f32[256]{0:T(256)}, u32[]{:S(2)}) copy-start(f32[256]{0:T(256)} %slice_reduce_fusion.3) | copy-start | bytes 3076
  360.7 262.8 %reduce-scatter.11.cloned.1.call-start = ((), (), s32[]{:S(2)}) async-start(), calls=%async_computation.11 | async-start | bytes 1966080 | tf_op jit(solution)/shard_map/reduce_scatter | solution.py:691
  363.6 105.5 %copy-start.56 = (f32[4,3,256]{2,1,0:T(4,128)S(1)}, f32[4,3,256]{2,1,0:T(4,128)}, u32[]{:S(2)}) copy-start(f32[4,3,256]{2,1,0:T(4,128)} %get-tuple-element.70) | copy-start | bytes 36868
  363.6 105.5 %copy-start.55 = (f32[768]{0:T(1024)S(1)}, f32[768]{0:T(1024)}, u32[]{:S(2)}) copy-start(f32[768]{0:T(1024)} %get-tuple-element.54) | copy-start | bytes 9220
  363.6 105.5 %copy-start.54 = (f32[768]{0:T(1024)S(1)}, f32[768]{0:T(1024)}, u32[]{:S(2)}) copy-start(f32[768]{0:T(1024)} %get-tuple-element.65) | copy-start | bytes 9220
  363.6 105.5 %copy-start.21 = (bf16[1024,768]{1,0:T(8,128)(2,1)S(1)}, bf16[1024,768]{1,0:T(8,128)(2,1)}, u32[]{:S(2)}) copy-start(bf16[1024,768]{1,0:T(8,128)(2,1)} %all-gather.9.cloned.1.call-done) | copy-start | bytes 4718596
  464.3 5.1 copy-start.60
  469.5 4.5 copy-start.27
  476.4 5.1 copy-start.1
  490.1 2.7 copy-start.36
  506.6 107.0 %copy-start.44 = (bf16[192,768]{1,0:T(8,128)(2,1)S(1)}, bf16[192,768]{1,0:T(8,128)(2,1)}, u32[]{:S(2)}) copy-start(bf16[192,768]{1,0:T(8,128)(2,1)} %get-tuple-element.49) | copy-start | bytes 884740
  606.1 9.6 %copy-start.11 = (bf16[768,576]{0,1:T(8,128)(2,1)S(1)}, bf16[768,576]{0,1:T(8,128)(2,1)}, u32[]{:S(2)}) copy-start(bf16[768,576]{0,1:T(8,128)(2,1)} %copy.137) | copy-start | bytes 2654212
  615.7 2.8 copy-start.33
  621.1 4.4 copy-start.41
  (23 other events, 43.2 us)
Sparse Core Ops, SparseCore 0:
  125.7 21.6 all-gather.4
  157.6 28.1 reduce-scatter.4
  190.4 19.6 all-gather.6
  246.5 28.1 reduce-scatter.6
  279.3 19.6 all-gather.8
  309.3 28.1 reduce-scatter.8
  360.8 20.6 all-gather.10
  496.8 26.5 reduce-scatter.10

commit v3 on v1

v3 whole, which is shorter than its diff:
```python
import functools

import jax
import jax.numpy as jnp
from jax import lax
from jax.experimental import pallas as pl
from jax.experimental.pallas import tpu as pltpu
from jax.sharding import PartitionSpec as P

HEAD = 64
norm_eps = 1e-05
MESH = pl.DeviceIdType.MESH
Y_SIZE = 2
Z_SIZE = 4
GROUP = Y_SIZE * Z_SIZE
F32 = jnp.float32
BF16 = jnp.bfloat16


class Place:
    def __init__(self):
        self.dp = lax.axis_index("dp")
        self.t = lax.axis_index("tensor")
        inner = lax.rem(self.dp, GROUP)
        base = self.dp - inner
        self.y = lax.rem(inner, Y_SIZE)
        self.z = inner // Y_SIZE
        z_pair = self.z + 1 - 2 * lax.rem(self.z, 2)
        z_mid = Z_SIZE - 1 - self.z
        self.is_end = jnp.logical_or(self.z == 0, self.z == Z_SIZE - 1)
        self.is_inner = jnp.logical_not(self.is_end)
        self.core = (self.dp, self.t + 1 - 2 * lax.rem(self.t, 2))
        self.over = (self.dp, lax.rem(self.t + 2, 4))
        self.diagonal = (self.dp, 3 - self.t)
        self.y_pair = (base + self.z * Y_SIZE + 1 - self.y, self.t)
        self.z_pair = (base + z_pair * Y_SIZE + self.y, self.t)
        self.z_right = (base + jnp.minimum(self.z + 1, Z_SIZE - 1) * Y_SIZE + self.y, self.t)
        self.z_left = (base + jnp.maximum(self.z - 1, 0) * Y_SIZE + self.y, self.t)
        self.z_mid = (base + z_mid * Y_SIZE + self.y, self.t)


class Links:
    def __init__(self, sems):
        self.sems = sems
        self.used = 0

    def copy(self, src, dst, device):
        at = self.used
        self.used += 1
        return pltpu.make_async_remote_copy(
            src_ref=src,
            dst_ref=dst,
            send_sem=self.sems.at[0, at],
            recv_sem=self.sems.at[1, at],
            device_id=device,
            device_id_type=MESH,
        )

    def again(self, src, dst, device):
        self.used -= 1
        return self.copy(src, dst, device)


def greet(devices):
    barrier = pltpu.get_barrier_semaphore()
    for device in devices:
        pl.semaphore_signal(barrier, inc=1, device_id=device, device_id_type=MESH)
    pl.semaphore_wait(barrier, len(devices))


def added(one, two, dtype):
    return (one.astype(F32) + two.astype(F32)).astype(dtype)


def small_item(place, links, mine, steps, landing, result):
    top = pl.ds(0, 8)
    steps[0] = mine[...]
    near = links.copy(steps.at[0, top], landing.at[0, top], place.core)
    near.start()
    yield
    near.wait_recv()
    steps[1] = steps[0]
    steps[1, top] = steps[0, top] + landing[0, top]
    over = links.copy(steps.at[1, top], landing.at[1, top], place.over)
    over.start()
    yield
    over.wait_recv()
    steps[2] = steps[1]
    steps[2, top] = steps[1, top] + landing[1, top]
    across = links.copy(steps.at[2], landing.at[2], place.y_pair)
    across.start()
    yield
    across.wait_recv()
    steps[3] = steps[2] + landing[2]
    pair_in = links.copy(steps.at[3], landing.at[3], place.z_pair)
    mid = links.copy(steps.at[4], landing.at[4], place.z_mid)
    pair_out = links.copy(result, landing.at[3], place.z_pair)

    @pl.when(place.is_end)
    def _():
        pair_in.start()

    yield

    @pl.when(place.is_inner)
    def _():
        pair_in.wait_recv()
        steps[4] = steps[3] + landing[3]
        mid.start()

    yield

    @pl.when(place.is_inner)
    def _():
        mid.wait_recv()
        result[...] = steps[4] + landing[4]
        pair_out.start()

    yield

    @pl.when(place.is_end)
    def _():
        pair_out.wait_recv()
        result[...] = landing[3]

    yield
    near.wait_send()
    over.wait_send()
    across.wait_send()

    @pl.when(place.is_end)
    def _():
        pair_in.wait_send()

    @pl.when(place.is_inner)
    def _():
        mid.wait_send()
        pair_out.wait_send()


class Ticker:
    def __init__(self):
        self.waiting = []
        self.running = []

    def add(self, items):
        self.waiting.extend(items)

    def tick(self, enter=1):
        for _ in range(enter):
            if self.waiting:
                self.running.append(self.waiting.pop(0))
        left = []
        for item in self.running:
            try:
                next(item)
                left.append(item)
            except StopIteration:
                pass
        self.running = left

    def finish(self):
        while self.waiting or self.running:
            self.tick()


def over_outer_groups(values):
    size = lax.axis_size("dp")
    if size == GROUP:
        return values
    groups = [[first + GROUP * turn for turn in range(size // GROUP)] for first in range(GROUP)]
    return [lax.psum(value, "dp", axis_index_groups=groups) for value in values]


def gelu_tanh(pre_active):
    return jax.nn.gelu(pre_active, approximate=True)


LANES = 128
SLOT = 256


def product(left, right, contract):
    return lax.dot_general(left, right, ((contract[:1], contract[1:]), ((), ())), preferred_element_type=F32)


def nn(left, right):
    return product(left, right, (1, 0))


def nt(left, right):
    return product(left, right, (1, 1))


def tn(left, right):
    return product(left, right, (0, 0))


class Gather:
    def __init__(self, place, links, rows):
        half = SLOT // 2
        self.near_copies, self.far_copies, self.pass_copies = [], [], []
        for part in range(2):
            own = pl.ds(part * half, half)
            beside = pl.ds(SLOT + part * half, half)
            over = pl.ds(2 * SLOT + part * half, half)
            diagonal = pl.ds(3 * SLOT + part * half, half)
            self.near_copies.append(links.copy(rows.at[own], rows.at[beside], place.core))
            self.far_copies.append(links.copy(rows.at[own], rows.at[over], place.over))
            self.pass_copies.append(links.copy(rows.at[over], rows.at[diagonal], place.core))

    def send(self, part):
        self.far_copies[part].start()
        self.near_copies[part].start()

    def near(self):
        for copy in self.near_copies:
            copy.wait_recv()

    def far(self, part):
        self.far_copies[part].wait_recv()
        self.pass_copies[part].start()

    def diagonal(self, part):
        self.pass_copies[part].wait_recv()

    def drain(self):
        for copy in self.near_copies + self.far_copies + self.pass_copies:
            copy.wait_send()


class Scatter:
    def __init__(self, place, links, rooms):
        self.core_out, self.core_in, self.far_out, self.far_in, self.near_out, self.near_in = rooms
        self.core_copies = [
            links.copy(self.core_out.at[part], self.core_in.at[part], place.core) for part in range(2)
        ]
        self.far_copies = [
            links.copy(self.far_out.at[part], self.far_in.at[part], place.over) for part in range(2)
        ]
        self.near_copies = [
            links.copy(self.near_out.at[part], self.near_in.at[part], place.core) for part in range(2)
        ]

    def beside(self, term):
        half = SLOT // 2
        for part in range(2):
            self.near_out[part] = term[part * half : (part + 1) * half].astype(BF16)
            self.near_copies[part].start()

    def diagonal(self, part, term):
        self.core_out[part] = term.astype(BF16)
        self.core_copies[part].start()

    def over(self, part, term):
        self.core_copies[part].wait_recv()
        self.far_out[part] = (term + self.core_in[part].astype(F32)).astype(BF16)
        self.far_copies[part].start()

    def arrived(self, part):
        self.near_copies[part].wait_recv()
        self.far_copies[part].wait_recv()
        return self.near_in[part].astype(F32) + self.far_in[part].astype(F32)

    def drain(self):
        for copy in self.core_copies + self.far_copies + self.near_copies:
            copy.wait_send()


def lane_masks():
    lane = lax.broadcasted_iota(jnp.int32, (1, LANES), 1)
    first = jnp.where(lane < HEAD, 1.0, 0.0).astype(BF16)
    return first, (1.0 - first.astype(F32)).astype(BF16)


def head_parts(tile, masks):
    parts = []
    width = tile.shape[-1]
    for first in range(0, width, LANES):
        piece = tile[:, first : min(first + LANES, width)]
        if piece.shape[-1] == HEAD:
            parts.append([piece])
        else:
            parts.append([piece * masks[0], piece * masks[1]])
    return parts


def whole_parts(tile):
    width = tile.shape[-1]
    return [tile[:, first : min(first + LANES, width)] for first in range(0, width, LANES)]


def allowed_rows(seg_cols, seg_rows, slot):
    return seg_cols[:, slot : slot + 1] == seg_rows[slot : slot + 1, :]


def attention_forward(query, keys, values, allowed):
    masks = lane_masks()
    outs = []
    for query_part, key_heads, value_heads in zip(
        whole_parts(query), head_parts(keys, masks), head_parts(values, masks)
    ):
        total = None
        for key_head, value_head in zip(key_heads, value_heads):
            scores = jnp.where(allowed, nt(query_part, key_head), -1000000000.0)
            grown = jnp.exp(scores - jnp.max(scores, axis=-1, keepdims=True))
            probs = grown * (1.0 / jnp.sum(grown, axis=-1, keepdims=True))
            term = nn(probs.astype(BF16), value_head)
            total = term if total is None else total + term
        outs.append(total.astype(BF16))
    return outs


def norm_rows(total, gain, shift):
    average = jnp.mean(total, axis=-1, keepdims=True)
    centered = total - average
    inverse = lax.rsqrt(jnp.mean(centered * centered, axis=-1, keepdims=True) + norm_eps)
    scaled = centered * inverse
    return scaled * gain + shift, scaled, inverse


OUT_BIAS, DOWN_BIAS, UP_BIAS, Q_BIAS, V_BIAS, GAIN, SHIFT = 0, 1, 2, 3, 4, 5, 7


def packed_inputs(segment_ids, qkv_weight, qv_bias, out_bias, norm_gain, norm_bias, up_bias, down_bias):
    own = lax.axis_index("tensor")
    order = jnp.stack([own, own ^ 1, own ^ 2, own ^ 3])
    seg_rows = segment_ids[order]
    layers, width, _, local = qkv_weight.shape
    padded = jnp.pad(qkv_weight, ((0, 0), (0, 0), (0, 0), (0, SLOT - local)))
    wide = lambda rows: jnp.pad(rows, ((0, 0), (0, 0), (0, width - rows.shape[-1])))
    small = jnp.concatenate(
        [
            out_bias[:, None],
            down_bias[:, None],
            wide(up_bias[:, None]),
            wide(qv_bias),
            norm_gain,
            norm_bias,
            jnp.zeros((layers, 7, width), BF16),
        ],
        axis=1,
    ).astype(F32)
    return seg_rows, seg_rows.T, small, padded.reshape(layers, width, 3 * SLOT)


def gelu_slope(raised):
    curve = (2.0 / jnp.pi) ** 0.5
    square = raised * raised
    bent = jnp.tanh(curve * raised * (1.0 + 0.044715 * square))
    return 0.5 * (1.0 + bent) + (0.5 * curve) * raised * (1.0 - bent * bent) * (1.0 + 0.134145 * square)


def attention_backward(query, keys, values, context_grad, allowed):
    masks = lane_masks()
    query_out, key_out, value_out = [], [], []
    for query_part, query_heads, key_heads, value_heads, grad_part, grad_heads in zip(
        whole_parts(query),
        head_parts(query, masks),
        head_parts(keys, masks),
        head_parts(values, masks),
        whole_parts(context_grad),
        head_parts(context_grad, masks),
    ):
        totals = None
        for query_head, key_head, value_head, grad_head in zip(
            query_heads, key_heads, value_heads, grad_heads
        ):
            scores = jnp.where(allowed, nt(key_head, query_part), -1000000000.0)
            grown = jnp.exp(scores - jnp.max(scores, axis=0, keepdims=True))
            probs = grown * (1.0 / jnp.sum(grown, axis=0, keepdims=True))
            probs_grad = nt(value_head, grad_part)
            shared = jnp.sum(probs_grad * probs, axis=0, keepdims=True)
            scores_grad = (probs * (probs_grad - shared)).astype(BF16)
            terms = (
                tn(scores_grad, key_head) * HEAD ** (-0.5),
                nn(scores_grad, query_head),
                nn(probs.astype(BF16), grad_head),
            )
            totals = terms if totals is None else tuple(map(jnp.add, totals, terms))
        query_out.append(totals[0].astype(BF16))
        key_out.append(totals[1].astype(BF16))
        value_out.append(totals[2].astype(BF16))
    return query_out, key_out, value_out


def norm_rows_backward(incoming, scaled, inverse, gain):
    inner = incoming * gain
    return inverse * (
        inner
        - jnp.mean(inner, axis=-1, keepdims=True)
        - scaled * jnp.mean(inner * scaled, axis=-1, keepdims=True)
    )


def column_sum(rows):
    return jnp.sum(rows.astype(F32), axis=0, keepdims=True)


def pair_item(place, links, mine, landing, result, local_sem, start, size):
    from_y, from_z, from_mid = landing
    half = size // 2
    here = pl.ds(pl.multiple_of(start + place.y * half, 16), half)
    there = pl.ds(pl.multiple_of(start + (1 - place.y) * half, 16), half)
    y_out = links.copy(mine.at[there], from_y, place.y_pair)
    pair_in = links.copy(mine.at[here], from_z, place.z_pair)
    mid = links.copy(mine.at[here], from_mid, place.z_mid)
    pair_out = links.copy(from_mid, from_z, place.z_pair)
    back_inner = links.copy(from_mid, result.at[here], place.y_pair)
    back_end = links.again(from_z, result.at[here], place.y_pair)
    keep_inner = pltpu.make_async_copy(from_mid, result.at[here], local_sem)
    keep_end = pltpu.make_async_copy(from_z, result.at[here], local_sem)
    y_out.start()
    yield
    y_out.wait_recv()
    mine[here] = added(mine[here], from_y[...], BF16)

    @pl.when(place.is_end)
    def _():
        pair_in.start()

    yield

    @pl.when(place.is_inner)
    def _():
        pair_in.wait_recv()
        mine[here] = added(mine[here], from_z[...], BF16)
        mid.start()

    yield

    @pl.when(place.is_inner)
    def _():
        mid.wait_recv()
        from_mid[...] = added(mine[here], from_mid[...], BF16)
        pair_out.start()
        back_inner.start()
        keep_inner.start()

    yield

    @pl.when(place.is_end)
    def _():
        pair_out.wait_recv()
        back_end.start()
        keep_end.start()

    yield
    yield
    back_inner.wait_recv()
    y_out.wait_send()

    @pl.when(place.is_end)
    def _():
        pair_in.wait_send()
        back_end.wait_send()
        keep_end.wait()

    @pl.when(place.is_inner)
    def _():
        mid.wait_send()
        pair_out.wait_send()
        back_inner.wait_send()
        keep_inner.wait()


def line_item(place, links, mine, landing, result, local_sem, start, size):
    from_left, from_right, from_y = landing
    quarter = size // Z_SIZE
    last = Z_SIZE - 1
    block = lambda at: pl.ds(start + at * quarter, quarter)
    own = pl.ds(pl.multiple_of(start + place.z * quarter, 16), quarter)
    right = {q: links.copy(mine.at[block(q)], from_left.at[q - 1], place.z_right) for q in range(1, Z_SIZE)}
    left = {q: links.copy(mine.at[block(q)], from_right.at[q], place.z_left) for q in range(last)}
    across = links.copy(mine.at[own], from_y, place.y_pair)
    go_right, go_left = [], []
    for distance in range(1, Z_SIZE):
        for copies, device, sign in ((go_right, place.z_right, 1), (go_left, place.z_left, -1)):
            at = place.z - sign * (distance - 1)
            rows = pl.ds(pl.multiple_of(start + jnp.clip(at, 0, last) * quarter, 16), quarter)
            source = from_y if distance == 1 else result.at[rows]
            copies.append(links.copy(source, result.at[rows], device))
    keep = pltpu.make_async_copy(from_y, result.at[own], local_sem)

    @pl.when(place.z == 0)
    def _():
        for q in range(last, 0, -1):
            right[q].start()

    @pl.when(place.z == last)
    def _():
        for q in range(last):
            left[q].start()

    yield
    for step in range(1, Z_SIZE):

        @pl.when(place.z == step)
        def _():
            for q in range(last, step - 1, -1):
                right[q].wait_recv()
                mine[block(q)] = added(mine[block(q)], from_left[q - 1], BF16)
                if q > step:
                    right[q].start()

        @pl.when(place.z == last - step)
        def _():
            for q in range(last - step + 1):
                left[q].wait_recv()
                mine[block(q)] = added(mine[block(q)], from_right[q], BF16)
                if q < last - step:
                    left[q].start()

        yield
    across.start()
    yield
    across.wait_recv()
    from_y[...] = added(mine[own], from_y[...], BF16)
    keep.start()

    @pl.when(place.z < last)
    def _():
        go_right[0].start()

    @pl.when(place.z > 0)
    def _():
        go_left[0].start()

    yield
    for distance in range(1, Z_SIZE):

        @pl.when(place.z >= distance)
        def _():
            go_right[distance - 1].wait_recv()

        if distance < last:

            @pl.when(jnp.logical_and(place.z >= distance, place.z < last))
            def _():
                go_right[distance].start()

        @pl.when(place.z <= last - distance)
        def _():
            go_left[distance - 1].wait_recv()

        if distance < last:

            @pl.when(jnp.logical_and(place.z <= last - distance, place.z > 0))
            def _():
                go_left[distance].start()

        yield
    across.wait_send()
    keep.wait()
    for q in range(1, Z_SIZE):

        @pl.when(place.z < q)
        def _():
            right[q].wait_send()

        @pl.when(place.z > last - q)
        def _():
            left[last - q].wait_send()

    for distance in range(1, Z_SIZE):

        @pl.when(jnp.logical_and(place.z >= distance - 1, place.z < last))
        def _():
            go_right[distance - 1].wait_send()

        @pl.when(jnp.logical_and(place.z <= last - distance + 1, place.z > 0))
        def _():
            go_left[distance - 1].wait_send()


def item_plan(rows):
    if rows % 768:
        return [(0, rows, False)]
    unit = rows // 768
    return [(0, 224 * unit, False), (448 * unit, 320 * unit, True), (224 * unit, 224 * unit, False)]


def item_rooms(rows, width):
    rooms = []
    for _, size, line in item_plan(rows):
        if line:
            rooms += [pltpu.VMEM((Z_SIZE - 1, size // Z_SIZE, width), BF16)] * 2
            rooms += [pltpu.VMEM((size // Z_SIZE, width), BF16)]
        else:
            rooms += [pltpu.VMEM((size // 2, width), BF16)] * 3
    return rooms


GAIN_ROW, SHIFT_ROW, OUT_BIAS_ROW, DOWN_BIAS_ROW, UP_BIAS_ROW, QV_BIAS_ROW = 0, 2, 4, 5, 8, 9
PARKED = ("full_in", "query", "keys", "values", "context", "full_mid", "pre", "active", "scaled", "inverse")


def whole_kernel(names, *refs):
    place = Place()
    ref = dict(zip(names, refs))
    links = Links(ref["sems"])
    small, state = ref["small"], ref["state"]
    full_in, query, keys, values, context = (ref[name] for name in PARKED[:5])
    full_mid, pre, active, scaled, inverse = (ref[name] for name in PARKED[5:])
    out_own, out_got = ref["out_own"], ref["out_got"]
    own_part, far_part, context_in = ref["own_part"], ref["far_part"], ref["context_in"]
    full_down, pre_grad, full_out, mixed_grad = (
        ref[name] for name in ("full_down", "pre_grad", "full_out", "mixed_grad")
    )
    layers = small.shape[0]
    local = query.shape[-1]
    half = SLOT // 2
    halves = [pl.ds(part * half, half) for part in range(2)]
    slots = [pl.ds(slot * SLOT, SLOT) for slot in range(4)]
    far_pieces = [
        [pl.ds(2 * SLOT + part * half, half), pl.ds(3 * SLOT + part * half, half)] for part in range(2)
    ]

    def vector(layer, row, width=small.shape[-1]):
        return small[layer, row : row + 1, :width]

    loads = {}
    at = 0
    for layer in range(layers):
        for name, target in (
            ("qkv", ref["qkv"].at[layer]),
            ("out", out_own.at[layer]),
            ("up", ref["up"].at[layer]),
            ("down", ref["down"].at[layer]),
        ):
            loads[layer, name] = pltpu.make_async_copy(
                ref[name + "_in"].at[layer], target, ref["load_sems"].at[at]
            )
            loads[layer, name].start()
            at += 1
    cotangent = pltpu.make_async_copy(ref["cotangent_in"], ref["cotangent"], ref["load_sems"].at[at])
    cotangent.start()
    greet((place.core, place.over, place.diagonal, place.y_pair, place.z_pair, place.z_mid))
    rooms = tuple(ref[name] for name in ("core_out", "core_in", "far_out", "far_in", "near_out", "near_in"))
    parks = {}

    def park(layer, these):
        for name in these:
            at = PARKED.index(name)
            parks[layer, name] = pltpu.make_async_copy(
                ref[name], ref["park_" + name].at[layer], ref["park_sems"].at[layer, 0, at]
            )
            parks[layer, name].start()

    def parked(layer, these):
        for name in these:
            if (layer, name) in parks:
                parks.pop((layer, name)).wait()

    def restore(layer, these):
        if layer < 0:
            return
        for name in these:
            at = PARKED.index(name)
            parks[layer, name] = pltpu.make_async_copy(
                ref["park_" + name].at[layer], ref[name], ref["park_sems"].at[layer, 1, at]
            )
            parks[layer, name].start()

    state[...] = ref["hidden"][...].astype(F32)
    gather = Gather(place, links, full_in)
    for part in range(2):
        full_in[halves[part]] = ref["hidden"][halves[part]]
        gather.send(part)
    mixed_grad[...] = jnp.zeros_like(mixed_grad)
    ref["small_grad"][...] = jnp.zeros_like(ref["small_grad"])
    drains = []
    for layer in range(layers):
        qkv_weight, up_weight, down_weight = ref["qkv"].at[layer], ref["up"].at[layer], ref["down"].at[layer]

        def attend(slot):
            rows = slots[slot]
            mixed = nn(full_in[rows], qkv_weight[...])
            query[rows] = ((mixed[:, :local] + vector(layer, Q_BIAS, local)) * HEAD ** (-0.5)).astype(BF16)
            keys[rows] = mixed[:, SLOT : SLOT + local].astype(BF16)
            values[rows] = (
                mixed[:, 2 * SLOT : 2 * SLOT + local] + vector(layer, V_BIAS, local)
            ).astype(BF16)
            outs = attention_forward(
                query[rows], keys[rows], values[rows],
                allowed_rows(ref["seg_cols"], ref["seg_rows"], slot),
            )
            first = 0
            for out in outs:
                context[rows, first : first + out.shape[-1]] = out
                first += out.shape[-1]

        sends = [
            links.copy(context.at[slots[slot]], context_in.at[slot - 1], device)
            for slot, device in ((1, place.core), (2, place.over), (3, place.diagonal))
        ]
        out_near = links.copy(out_own.at[layer], out_got.at[0], place.core)
        out_far = links.copy(out_own.at[layer], out_got.at[1], place.over)
        out_pass = links.copy(out_got.at[1], out_got.at[2], place.core)
        loads[layer, "out"].wait()
        out_near.start()
        loads[layer, "qkv"].wait()
        parked(layer - 1, PARKED)
        attend(0)
        gather.near()
        attend(1)
        sends[0].start()
        gather.far(0)
        gather.far(1)
        out_far.start()
        gather.diagonal(0)
        gather.diagonal(1)
        attend(2)
        sends[1].start()
        out_far.wait_recv()
        out_pass.start()
        attend(3)
        sends[2].start()
        own_part[...] = nn(context[slots[0]], out_own[layer])
        out_near.wait_recv()
        sends[0].wait_recv()
        own_part[...] += nn(context_in[0], out_got[0])
        out_pass.wait_recv()
        sends[1].wait_recv()
        sends[2].wait_recv()
        gather.drain()
        for copy in sends + [out_near, out_far, out_pass]:
            copy.wait_send()
        if layer < layers - 1:
            park(layer, PARKED[:5])
        gather = Gather(place, links, full_mid)
        for part in range(2):
            rows = halves[part]
            total = (
                own_part[rows]
                + nn(context_in[1, rows], out_got[1])
                + nn(context_in[2, rows], out_got[2])
                + state[rows]
                + vector(layer, OUT_BIAS)
            )
            normed, scaled_part, inverse_part = norm_rows(total, vector(layer, GAIN), vector(layer, SHIFT))
            full_mid[rows] = normed.astype(BF16)
            gather.send(part)
            state[rows] = normed
            scaled[0, rows] = scaled_part
            inverse[0, rows] = jnp.broadcast_to(inverse_part, (half, LANES))
        loads[layer, "up"].wait()
        loads[layer, "down"].wait()
        scatter = Scatter(place, links, rooms)

        def feed(pieces):
            rows_in = jnp.concatenate([full_mid[piece] for piece in pieces])
            size = rows_in.shape[0] // len(pieces)
            for first in range(0, up_weight.shape[-1], SLOT):
                columns = slice(first, first + SLOT)
                raised = nn(rows_in, up_weight[:, columns]) + small[layer, UP_BIAS : UP_BIAS + 1, columns]
                shaped = gelu_tanh(raised).astype(BF16)
                for at, piece in enumerate(pieces):
                    pre[piece, columns] = raised[at * size : (at + 1) * size]
                    active[piece, columns] = shaped[at * size : (at + 1) * size]
            return nn(jnp.concatenate([active[piece] for piece in pieces]), down_weight[...])

        own_part[...] = feed([slots[0]])
        gather.near()
        parked(layer, PARKED[:5])
        scatter.beside(feed([slots[1]]))
        for part in range(2):
            gather.far(part)
            gather.diagonal(part)
            far_part[...] = feed(far_pieces[part])
            scatter.diagonal(part, far_part[half:])
            scatter.over(part, far_part[:half])
        gather.drain()
        if layer < layers - 1:
            gather = Gather(place, links, full_in)
        for part in range(2):
            rows = halves[part]
            total = state[rows] + own_part[rows] + scatter.arrived(part) + vector(layer, DOWN_BIAS)
            normed, scaled_part, inverse_part = norm_rows(
                total, vector(layer, GAIN + 1), vector(layer, SHIFT + 1)
            )
            state[rows] = normed
            if layer < layers - 1:
                full_in[rows] = normed.astype(BF16)
                gather.send(part)
            else:
                ref["result"][rows] = normed.astype(BF16)
            scaled[1, rows] = scaled_part
            inverse[1, rows] = jnp.broadcast_to(inverse_part, (half, LANES))
        scatter.drain()
        if layer < layers - 1:
            park(layer, PARKED[5:])

    ticker = Ticker()
    item_count = 0

    def sum_items(layer, name):
        nonlocal item_count
        mine = ref[name + "_grad"].at[layer]
        items = []
        for at, (start, size, line) in enumerate(item_plan(mine.shape[0])):
            landing = tuple(ref[f"land_{name}_{layer}_{at}_{room}"] for room in range(3))
            make = line_item if line else pair_item
            items.append(
                make(
                    place, links, mine, landing, ref[name + "_sum"].at[layer],
                    ref["item_sems"].at[item_count], start, size,
                )
            )
            item_count += 1
        return items

    cotangent.wait()
    state[...] = ref["cotangent"][...].astype(F32)
    for layer in reversed(range(layers)):
        qkv_weight, up_weight, down_weight = ref["qkv"].at[layer], ref["up"].at[layer], ref["down"].at[layer]
        small_grad = ref["small_grad"].at[layer]

        def norm_step(at, part, bias_row, target):
            rows = halves[part]
            incoming, scaled_part = state[rows], scaled[at, rows]
            small_grad[GAIN_ROW + at : GAIN_ROW + at + 1] += column_sum(incoming * scaled_part)
            small_grad[SHIFT_ROW + at : SHIFT_ROW + at + 1] += column_sum(incoming)
            total = norm_rows_backward(incoming, scaled_part, inverse[at, rows][:, :1], vector(layer, GAIN + at))
            state[rows] = total
            low = total.astype(BF16)
            target[rows] = low
            gather.send(part)
            small_grad[bias_row : bias_row + 1] += column_sum(low)

        parked(layer, ("scaled", "inverse"))
        gather = Gather(place, links, full_down)
        scatter = Scatter(place, links, rooms)
        for part in range(2):
            norm_step(1, part, DOWN_BIAS_ROW, full_down)
        parked(layer, PARKED)

        def feed_back(pieces):
            rows_in = jnp.concatenate([full_down[piece] for piece in pieces])
            size = rows_in.shape[0] // len(pieces)
            for first in range(0, up_weight.shape[-1], SLOT):
                columns = slice(first, first + SLOT)
                raised = jnp.concatenate([pre[piece, columns] for piece in pieces])
                low = (nt(rows_in, down_weight[columns]) * gelu_slope(raised)).astype(BF16)
                small_grad[UP_BIAS_ROW : UP_BIAS_ROW + 1, columns] += column_sum(low)
                for at, piece in enumerate(pieces):
                    pre_grad[piece, columns] = low[at * size : (at + 1) * size]
            return nt(jnp.concatenate([pre_grad[piece] for piece in pieces]), up_weight[...])

        own_part[...] = feed_back([slots[0]])
        gather.near()
        ticker.tick()
        scatter.beside(feed_back([slots[1]]))
        for part in range(2):
            gather.far(part)
            gather.diagonal(part)
            far_part[...] = feed_back(far_pieces[part])
            scatter.diagonal(part, far_part[half:])
            scatter.over(part, far_part[:half])
            ticker.tick()
        gather.drain()

        def weight_grad(name, left, right, columns=None):
            target = ref[name + "_grad"].at[layer]
            for first in range(0, left.shape[-1], SLOT):
                last = min(first + SLOT, left.shape[-1])
                target[first:last] = tn(left[:, first:last], right[...]).astype(BF16)

        weight_grad("down", active, full_down)
        ticker.add(sum_items(layer, "down"))
        ticker.tick(3)
        weight_grad("up", full_mid, pre_grad)
        ticker.add(sum_items(layer, "up"))
        restore(layer - 1, ("full_mid", "pre", "active"))
        ticker.tick()
        for part in range(2):
            rows = halves[part]
            state[rows] = state[rows] + own_part[rows] + scatter.arrived(part)
        scatter.drain()
        gather = Gather(place, links, full_out)
        scatter = Scatter(place, links, rooms)
        for part in range(2):
            norm_step(0, part, OUT_BIAS_ROW, full_out)
        restore(layer - 1, ("scaled", "inverse"))

        def attend_back(slot):
            rows = slots[slot]
            context_grad = nt(full_out[rows], out_own[layer]).astype(BF16)
            outs = attention_backward(
                query[rows], keys[rows], values[rows], context_grad,
                allowed_rows(ref["seg_cols"], ref["seg_rows"], slot),
            )
            for at, parts in enumerate(outs):
                first = at * SLOT
                for out in parts:
                    mixed_grad[rows, first : first + out.shape[-1]] = out
                    first += out.shape[-1]
            return nt(mixed_grad[rows], qkv_weight[...])

        own_part[...] = attend_back(0)
        ticker.tick()
        gather.near()
        scatter.beside(attend_back(1))
        gather.far(0)
        ticker.tick()
        gather.far(1)
        far_part[...] = attend_back(2)
        gather.diagonal(0)
        gather.diagonal(1)
        ticker.tick()
        term = attend_back(3)
        for part in range(2):
            scatter.diagonal(part, term[part * half : (part + 1) * half])
        for part in range(2):
            scatter.over(part, far_part[halves[part]])
        gather.drain()
        ticker.tick()
        weight_grad("out", context, full_out)
        for first in range(0, full_in.shape[-1], SLOT):
            rows = pl.ds(first, SLOT)
            mixed = tn(full_in[:, first : first + SLOT], mixed_grad[...]).astype(BF16)
            for at in range(3):
                ref["qkv_grad"][layer, rows, at * local : (at + 1) * local] = mixed[
                    :, at * SLOT : at * SLOT + local
                ]
        sums = column_sum(mixed_grad[...])
        for row, first in ((QV_BIAS_ROW, 0), (QV_BIAS_ROW + 1, 2 * SLOT)):
            small_grad[row : row + 1, :SLOT] = sums[:, first : first + SLOT]
        ticker.add(sum_items(layer, "qkv"))
        ticker.add(sum_items(layer, "out"))
        ticker.add(
            [
                small_item(
                    place, links, small_grad, ref["small_steps"].at[layer], ref["small_land"].at[layer],
                    ref["small_sum"].at[layer],
                )
            ]
        )
        restore(layer - 1, PARKED[:5])
        for part in range(2):
            rows = halves[part]
            state[rows] = state[rows] + own_part[rows] + scatter.arrived(part)
        scatter.drain()
        ticker.tick()
    ref["hidden_grad"][...] = state[...]
    ticker.tick(6)
    ticker.finish()


def run_whole(hidden, cotangent, seg_rows, seg_cols, small, qkv, out, up, down):
    layers, width, wide = qkv.shape
    local, hidden_units = out.shape[1], up.shape[-1]
    rows = hidden.shape[0]
    group, half = 4 * rows, rows // 2
    vmem = pl.BlockSpec(memory_space=pltpu.VMEM)
    anywhere = pl.BlockSpec(memory_space=pl.ANY)
    inputs = [
        ("hidden", hidden, vmem),
        ("seg_rows", seg_rows, vmem),
        ("seg_cols", seg_cols, vmem),
        ("small", small, vmem),
        ("cotangent_in", cotangent, anywhere),
        ("qkv_in", qkv, anywhere),
        ("out_in", out, anywhere),
        ("up_in", up, anywhere),
        ("down_in", down, anywhere),
    ]
    saved = [
        ((group, width), BF16),
        ((group, local), BF16),
        ((group, local), BF16),
        ((group, local), BF16),
        ((group, local), BF16),
        ((group, width), BF16),
        ((group, hidden_units), F32),
        ((group, hidden_units), BF16),
        ((2, rows, width), F32),
        ((2, rows, LANES), F32),
    ]
    grads = {
        "down": (hidden_units, width),
        "up": (width, hidden_units),
        "qkv": (width, 3 * local),
        "out": (local, width),
    }
    outputs = [
        ("result", (rows, width), BF16, vmem),
        ("hidden_grad", (rows, width), F32, vmem),
        ("small_sum", (layers, 16, width), F32, vmem),
    ]
    outputs += [(name + "_sum", (layers,) + shape, BF16, anywhere) for name, shape in grads.items()]
    outputs += [
        ("park_" + name, (layers - 1,) + shape, dtype, anywhere)
        for name, (shape, dtype) in zip(PARKED, saved)
    ]
    scratch = [(name, pltpu.VMEM(shape, dtype)) for name, (shape, dtype) in zip(PARKED, saved)]
    scratch += [
        ("cotangent", pltpu.VMEM((rows, width), BF16)),
        ("qkv", pltpu.VMEM(qkv.shape, BF16)),
        ("out_own", pltpu.VMEM(out.shape, BF16)),
        ("out_got", pltpu.VMEM((3,) + out.shape[1:], BF16)),
        ("up", pltpu.VMEM(up.shape, BF16)),
        ("down", pltpu.VMEM(down.shape, BF16)),
        ("context_in", pltpu.VMEM((3, rows, local), BF16)),
        ("own_part", pltpu.VMEM((rows, width), F32)),
        ("far_part", pltpu.VMEM((rows, width), F32)),
        ("state", pltpu.VMEM((rows, width), F32)),
        ("full_down", pltpu.VMEM((group, width), BF16)),
        ("pre_grad", pltpu.VMEM((group, hidden_units), BF16)),
        ("full_out", pltpu.VMEM((group, width), BF16)),
        ("mixed_grad", pltpu.VMEM((group, wide), BF16)),
        ("small_grad", pltpu.VMEM((layers, 16, width), F32)),
        ("small_steps", pltpu.VMEM((layers, 5, 16, width), F32)),
        ("small_land", pltpu.VMEM((layers, 5, 16, width), F32)),
    ]
    scratch += [
        (name, pltpu.VMEM((2, half, width), BF16))
        for name in ("core_out", "core_in", "far_out", "far_in", "near_out", "near_in")
    ]
    items = 0
    for name, shape in grads.items():
        scratch.append((name + "_grad", pltpu.VMEM((layers,) + shape, BF16)))
        for layer in range(layers):
            items += len(item_plan(shape[0]))
            scratch += [
                (f"land_{name}_{layer}_{at // 3}_{at % 3}", room)
                for at, room in enumerate(item_rooms(*shape))
            ]
    scratch += [
        ("load_sems", pltpu.SemaphoreType.DMA((4 * layers + 1,))),
        ("park_sems", pltpu.SemaphoreType.DMA((layers, 2, len(PARKED)))),
        ("item_sems", pltpu.SemaphoreType.DMA((items,))),
        ("sems", pltpu.SemaphoreType.DMA((2, 320))),
    ]
    names = [entry[0] for entry in inputs + outputs + scratch]
    done = pl.pallas_call(
        functools.partial(whole_kernel, names),
        out_shape=[jax.ShapeDtypeStruct(shape, dtype) for _, shape, dtype, _ in outputs],
        in_specs=[spec for _, _, spec in inputs],
        out_specs=[spec for _, _, _, spec in outputs],
        scratch_shapes=[room for _, room in scratch],
        compiler_params=pltpu.CompilerParams(
            collective_id=0, has_side_effects=True, vmem_limit_bytes=62 << 20
        ),
    )(*[array for _, array, _ in inputs])
    return done[: 3 + len(grads)]


def on_device(
    hidden_in,
    segment_ids,
    out_cotangent,
    qkv_weight,
    qv_bias,
    out_weight,
    out_bias,
    norm_gain,
    norm_bias,
    up_weight,
    up_bias,
    down_weight,
    down_bias,
):
    layers, width, _, local = qkv_weight.shape
    seg_rows, seg_cols, small, qkv_wide = packed_inputs(
        segment_ids, qkv_weight, qv_bias, out_bias, norm_gain, norm_bias, up_bias, down_bias
    )
    result, hidden_grad, *sums = run_whole(
        hidden_in, out_cotangent, seg_rows, seg_cols, small, qkv_wide, out_weight, up_weight, down_weight
    )
    sums = over_outer_groups(sums)
    small_sum, down, up, qkv, out = sums
    return (
        result,
        hidden_grad,
        qkv.reshape(layers, width, 3, local).astype(F32),
        small_sum[:, QV_BIAS_ROW : QV_BIAS_ROW + 2, :local],
        out.astype(F32),
        small_sum[:, OUT_BIAS_ROW],
        small_sum[:, GAIN_ROW : GAIN_ROW + 2],
        small_sum[:, SHIFT_ROW : SHIFT_ROW + 2],
        up.astype(F32),
        small_sum[:, UP_BIAS_ROW, : up_bias.shape[-1]],
        down.astype(F32),
        small_sum[:, DOWN_BIAS_ROW],
    )


def solution(mesh):
    placed = (
        P(("dp", "tensor"), None),
        P("dp", None),
        P(("dp", "tensor"), None),
        P(None, None, None, "tensor"),
        P(None, None, "tensor"),
        P(None, "tensor", None),
        P(),
        P(),
        P(),
        P(None, None, "tensor"),
        P(None, "tensor"),
        P(None, "tensor", None),
        P(),
    )
    return jax.shard_map(
        on_device,
        mesh=mesh,
        in_specs=placed,
        out_specs=(
            P(("dp", "tensor"), None),
            P(("dp", "tensor"), None),
            P(None, None, None, "tensor"),
            P(None, None, "tensor"),
            P(None, "tensor", None),
            P(),
            P(),
            P(),
            P(None, None, "tensor"),
            P(None, "tensor"),
            P(None, "tensor", None),
            P(),
        ),
        check_vma=False,
    )
```

time: 729 us -> 341 us (0.47)
  waiting for transfers between devices: 279 us -> 0 us
  Pallas kernels: 199 us -> 305 us
  matrix products: 95.4 us -> 0 us
  local copies, waits for them, and re-layouts: 70.6 us -> 21.2 us
  other arithmetic: 51.1 us -> 7.99 us
  between operations: 15.3 us -> 0.89 us
  starting transfers between devices: 9.87 us -> 0 us
    all_gather x10 -> x0, waiting for transfers between devices: 136 us -> none  [the longest x4 78.8 us: spread_rows(): return lax.all_gather(shard, 'tensor', axis=0, tiled=True)]
    reduce_scatter x6 -> x0, waiting for transfers between devices: 128 us -> none  [the longest x4 71.6 us: sum_backward(): lax.psum_scatter(partial_value(jnp.int32(0), my_rows * lax.axis_size('ten...]
    pallas_call x2 -> x1, Pallas kernels: 199 us -> 305 us  [run_whole(): pl.pallas_call(functools.partial(whole_kernel, names), out_shape=[jax.Sha...]
    dot_general x35 -> x0, matrix products: 93.1 us -> none  [the longest x4 12.8 us: partial_value(): jnp.einsum('nf,df->nd', full, weight, preferred_element_type=jnp.float32)]
    reduce_sum x20 -> x0, other arithmetic: 15.8 us -> none  [the longest x4 7.12 us: norm_backward(): gain_grad = jnp.sum(incoming * scaled, axis=0)]
    another operation x13 -> x0, other arithmetic: 14.3 us -> none  [the longest x10 12.9 us: final_sums(): jnp.stack([summed[layer_index][member] for layer_index in range(len(summe...]
    all_to_all x2 -> x0, waiting for transfers between devices: 13.5 us -> none  [project_rows(): lax.all_to_all(context, 'tensor', split_axis=0, concat_axis=1, tiled=True)]
    unnamed x108 -> x16, local copies, waits for them, and re-layouts: 14.7 us -> 3.43 us
  transfers between devices with their start and end apart: 18 -> 0, of which waited for: 15 -> 0; matrix products, arithmetic and copies ran while one was open for 14% -> 0% of each run, Pallas kernels for 28% -> 0%
where the time goes in v3:
time: 341 us; the launch traced here: 335 us
  Pallas kernels  305 us (89%)
  local copies, waits for them, and re-layouts  21.2 us (6%)
  other arithmetic  7.99 us (2%)
    pallas_call x1, Pallas kernels, run_whole(): pl.pallas_call(functools.partial(whole_kernel, names), out_shape=[jax.Sha...  305 us

profile of v3, /device:TPU:0, one launch (start us, length us, event | category | flops | bytes accessed | tf_op | source)
XLA Modules:
  0.0 335.2 jit_solution(17950681910791382630)
XLA Ops:
  0.6 0.0 copy-start
  0.7 0.1 fusion
  0.8 0.6 copy-done
  1.3 0.6 gather_fusion
  1.9 0.0 copy-start.5
  1.9 0.7 pad.8
  2.6 0.7 copy.29
  3.3 0.7 copy.31
  4.0 0.7 copy.30
  4.7 1.6 concatenate.22
  6.3 0.6 convert_element_type.22.refs_3_
  6.9 0.8 copy.28
  7.7 1.6 pad.9
  9.4 2.4 copy.32.refs_5_
  11.8 0.0 copy-done.5
  11.8 305.1 %shard_map.220 = (bf16[256,768]{1,0:T(8,128)(2,1)}, f32[256,768]{1,0:T(8,128)}, f32[2,16,768]{2,1,0:T(8,128)}, bf16[2,768,768]{2,1,0:T(8,128)(2,1)}, bf16[2,768,...) custom-call(bf16[256,768]{1,0:T(8,128)(2,1)} %refs_0_.1, ...), custom_call_target="tpu_custom_call" | custom-call | tf_op jit(solution)/shard_map/pallas_call | solution.py:1036
  316.9 1.3 slice.18
  318.2 0.9 fusion.1
  319.1 1.5 fusion.2
  320.6 0.6 copy_bitcast_fusion
  321.2 0.6 copy.40
  321.8 2.2 convert_element_type.25
  324.0 0.0 copy-start.2
  324.0 4.3 %copy.33 = f32[2,768,576]{1,2,0:T(8,128)} copy(bf16[2,768,576]{2,1,0:T(8,128)(2,1)} %get-tuple-element.21) | data formatting | bytes 5308416 | tf_op jit(solution)/shard_map/convert_element_type | solution.py:1076
  328.3 0.0 copy-done.2
  328.3 0.0 copy-start.1
  328.3 2.5 convert_element_type.26
  330.8 0.0 copy-done.1
  330.8 0.0 copy-start.4
  330.8 0.0 copy-start.3
  330.8 2.5 convert_element_type.27
  333.4 0.0 copy-done.4
  333.4 0.7 copy.43
  334.1 0.0 copy-done.3
  334.1 0.9 copy.44
  (2 shorter events, 0.0 us)
Async XLA Ops:
  0.6 0.7 copy-start
  1.9 9.9 %copy-start.5 = (s32[4,256]{1,0:T(4,128)}, s32[4,256]{1,0:T(4,128)S(1)}, u32[]{:S(2)}) copy-start(s32[4,256]{1,0:T(4,128)S(1)} %gather_fusion) | copy-start | bytes 12292
  324.0 4.3 %copy-start.2 = (bf16[2,768,768]{2,1,0:T(8,128)(2,1)S(1)}, bf16[2,768,768]{2,1,0:T(8,128)(2,1)}, u32[]{:S(2)}) copy-start(bf16[2,768,768]{2,1,0:T(8,128)(2,1)} %get-tuple-element.24) | copy-start | bytes 7077892
  328.3 2.6 copy-start.1
  330.8 2.6 copy-start.4
  330.8 3.3 copy-start.3
